TPU v7x, 32 devices: a whole 2x2x4 slice. The times are simulated.
32 devices in a mesh: img: 4 (over y, x), seq: 8 (over z, core).
Axes of the slice: x: 2, y: 2, z: 4, core: 2. Of those that a mesh axis runs over, the one named last changes fastest.
Arguments:
- patches: bfloat16 [20, 1024, 768], P('img', 'seq'), may hold values from -6 to 6
- counts: int32 [20], P('img'), may hold values from 128 to 1024, as said below
- norm_gain_one: bfloat16 [768], replicated, may hold values from 0.099609375 to 1.8984375
- w_query: bfloat16 [768, 768], replicated, may hold values from -0.21875 to 0.21875
- w_key: bfloat16 [768, 768], replicated, may hold values from -0.21875 to 0.21875
- w_value: bfloat16 [768, 768], replicated, may hold values from -0.21875 to 0.21875
- w_out: bfloat16 [768, 768], replicated, may hold values from -3.5 to 3.5
- norm_gain_two: bfloat16 [768], replicated, may hold values from 0.099609375 to 1.8984375
- w_gate: bfloat16 [768, 2048], replicated, may hold values from -0.21875 to 0.21875
- w_up: bfloat16 [768, 2048], replicated, may hold values from -0.21875 to 0.21875
- w_down: bfloat16 [2048, 768], replicated, may hold values from -0.125 to 0.125
- cotangent: bfloat16 [20, 1024, 768], P('img', 'seq'), may hold values from -6 to 6
Outputs:
- layer_out: bfloat16 [20, 1024, 768], P('img', 'seq')
- grad_input: bfloat16 [20, 1024, 768], P('img', 'seq')
- grad_gain_one: float32 [768], replicated
- grad_w_query: float32 [768, 768], replicated
- grad_w_key: float32 [768, 768], replicated
- grad_w_value: float32 [768, 768], replicated
- grad_w_out: float32 [768, 768], replicated
- grad_gain_two: float32 [768], replicated
- grad_w_gate: float32 [768, 2048], replicated
- grad_w_up: float32 [768, 2048], replicated
- grad_w_down: float32 [2048, 768], replicated
- rms_stats: float32 [4], replicated
Inputs may be any that keep to these rules, and one draw needn't show every extreme that they name: The valid patches of chart c are its first counts[c] positions. In every run of 5 charts that share an index of img, one chart, drawn from the seed, has all 1024 patches valid.
All inputs are finite; a program needn't handle non-finite values.
Results may differ from a plain program's by a relative error of at most 0.019.
Values may be sent and summed in bfloat16 or wider, within the bound.
No kernel may reach another device: no remote copies, remote signals or barrier semaphores. Data moves between devices by JAX's collectives and lax.ppermute only.
A program may use at most 384 MiB of HBM per device.

v0:
```python
import jax
import jax.numpy as jnp
from jax import lax
from jax.sharding import PartitionSpec as P

HEADS = 12


eps_norm = 1e-06
big_negative = -1000000000.0
start_max = -1e30
score_scale = 0.125


def rms_scale(values_in, gain_vec):
    return (
        values_in
        * lax.rsqrt(jnp.mean(values_in * values_in, axis=-1, keepdims=True) + eps_norm)
        * gain_vec
    )


def mlp_core(gate_in, up_in):
    return jax.nn.gelu(gate_in, approximate=True) * up_in


def masked_squares(values_in, row_mask):
    return jnp.sum(row_mask * jnp.sum(values_in * values_in, axis=-1))


def score_grads(query_one, key_split, value_split, valid_one, log_one, delta_one, grad_one):
    scores = (
        jnp.einsum("qhd,khd->hqk", query_one, key_split, preferred_element_type=jnp.float32)
        * score_scale
    )
    scores = jnp.where(valid_one[None, None, :], scores, big_negative)
    probs = jnp.exp(scores - log_one[:, :, None])
    grad_probs = jnp.einsum(
        "qhd,khd->hqk", grad_one, value_split, preferred_element_type=jnp.float32
    )
    grad_scores = (probs * (grad_probs - delta_one[:, :, None])).astype(jnp.bfloat16)
    return (grad_scores, probs.astype(jnp.bfloat16))


def body(
    patches,
    counts,
    norm_gain_one,
    w_query,
    w_key,
    w_value,
    w_out,
    norm_gain_two,
    w_gate,
    w_up,
    w_down,
    cotangent,
):
    charts, block_len, model_width = patches.shape
    head_dim = model_width // HEADS
    row_total = charts * block_len
    positions = lax.axis_index("seq") * block_len + lax.iota(jnp.int32, block_len)
    row_valid = positions[None, :] < counts[:, None]
    row_mask = row_valid.reshape(row_total).astype(jnp.float32)
    resid_in = patches.astype(jnp.float32).reshape(row_total, model_width)
    gain_one = norm_gain_one.astype(jnp.float32)
    gain_two = norm_gain_two.astype(jnp.float32)
    first_in = rms_scale(resid_in, gain_one).astype(jnp.bfloat16)
    query_rows = jnp.dot(first_in, w_query, preferred_element_type=jnp.float32).astype(jnp.bfloat16)
    key_rows = jnp.dot(first_in, w_key, preferred_element_type=jnp.float32).astype(jnp.bfloat16)
    value_rows = jnp.dot(first_in, w_value, preferred_element_type=jnp.float32).astype(jnp.bfloat16)
    query_heads = query_rows.reshape(charts, block_len, HEADS, head_dim)
    key_blocks = key_rows.reshape(charts, block_len, model_width)
    value_blocks = value_rows.reshape(charts, block_len, model_width)
    start_state = (
        jnp.full((charts, HEADS, block_len), start_max, jnp.float32),
        jnp.zeros((charts, HEADS, block_len), jnp.float32),
        jnp.zeros((charts, HEADS, block_len, head_dim), jnp.float32),
    )
    key_piece = lax.all_gather(key_blocks, "seq", axis=1, tiled=True)
    value_piece = lax.all_gather(value_blocks, "seq", axis=1, tiled=True)
    piece_len = key_piece.shape[1]
    key_valid = lax.iota(jnp.int32, piece_len)[None, :] < counts[:, None]

    def attend_per_chart(bundle):
        run_max, run_sum, run_acc, query_one, key_one, value_one, valid_one = bundle
        key_split = key_one.reshape(piece_len, HEADS, head_dim)
        value_split = value_one.reshape(piece_len, HEADS, head_dim)
        scores = (
            jnp.einsum("qhd,khd->hqk", query_one, key_split, preferred_element_type=jnp.float32)
            * score_scale
        )
        scores = jnp.where(valid_one[None, None, :], scores, big_negative)
        new_max = jnp.maximum(run_max, jnp.max(scores, axis=-1))
        factor = jnp.exp(run_max - new_max)
        weights = jnp.exp(scores - new_max[:, :, None])
        new_sum = run_sum * factor + jnp.sum(weights, axis=-1)
        new_acc = run_acc * factor[:, :, None] + jnp.einsum(
            "hqk,khd->hqd",
            weights.astype(jnp.bfloat16),
            value_split,
            preferred_element_type=jnp.float32,
        )
        return (new_max, new_sum, new_acc)

    run_max, run_sum, run_acc = lax.map(
        attend_per_chart,
        (
            start_state[0],
            start_state[1],
            start_state[2],
            query_heads,
            key_piece,
            value_piece,
            key_valid,
        ),
    )
    attn_heads = run_acc / run_sum[:, :, :, None]
    log_total = run_max + jnp.log(run_sum)
    attn_trans = jnp.transpose(attn_heads, (0, 2, 1, 3))
    attn_rows = attn_trans.reshape(row_total, model_width)
    attn_in = attn_rows.astype(jnp.bfloat16)
    branch_one = jnp.dot(attn_in, w_out, preferred_element_type=jnp.float32)
    middle = resid_in + branch_one
    second_in = rms_scale(middle, gain_two).astype(jnp.bfloat16)
    gate_rows = jnp.dot(second_in, w_gate, preferred_element_type=jnp.float32)
    up_rows = jnp.dot(second_in, w_up, preferred_element_type=jnp.float32)
    inner = mlp_core(gate_rows, up_rows).astype(jnp.bfloat16)
    branch_two = jnp.dot(inner, w_down, preferred_element_type=jnp.float32)
    result = middle + branch_two
    squares = jnp.stack(
        [
            masked_squares(resid_in, row_mask),
            masked_squares(branch_one, row_mask),
            masked_squares(branch_two, row_mask),
            masked_squares(result, row_mask),
        ]
    )
    valid_count = jnp.sum(row_mask)
    grad_low = cotangent.reshape(row_total, model_width)
    grad_out = grad_low.astype(jnp.float32)
    grad_w_down = jnp.dot(inner.T, grad_low, preferred_element_type=jnp.float32)
    grad_inner = jnp.dot(grad_low, w_down.T, preferred_element_type=jnp.float32)
    _, mlp_back = jax.vjp(mlp_core, gate_rows, up_rows)
    grad_gate, grad_up = mlp_back(grad_inner)
    grad_gate = grad_gate.astype(jnp.bfloat16)
    grad_up = grad_up.astype(jnp.bfloat16)
    grad_w_gate = jnp.dot(second_in.T, grad_gate, preferred_element_type=jnp.float32)
    grad_w_up = jnp.dot(second_in.T, grad_up, preferred_element_type=jnp.float32)
    grad_second = jnp.dot(grad_gate, w_gate.T, preferred_element_type=jnp.float32) + jnp.dot(
        grad_up, w_up.T, preferred_element_type=jnp.float32
    )
    _, norm_back_two = jax.vjp(rms_scale, middle, gain_two)
    grad_mid_norm, grad_gain_two = norm_back_two(grad_second)
    grad_mid = grad_out + grad_mid_norm
    grad_mid_low = grad_mid.astype(jnp.bfloat16)
    grad_w_out = jnp.dot(attn_in.T, grad_mid_low, preferred_element_type=jnp.float32)
    grad_attn = jnp.dot(grad_mid_low, w_out.T, preferred_element_type=jnp.float32).astype(
        jnp.bfloat16
    )
    grad_heads = grad_attn.reshape(charts, block_len, HEADS, head_dim)
    delta = jnp.transpose(jnp.sum(grad_heads.astype(jnp.float32) * attn_trans, axis=-1), (0, 2, 1))
    key_piece = lax.all_gather(key_blocks, "seq", axis=1, tiled=True)
    value_piece = lax.all_gather(value_blocks, "seq", axis=1, tiled=True)
    back_piece_len = key_piece.shape[1]
    key_valid = lax.iota(jnp.int32, back_piece_len)[None, :] < counts[:, None]

    def back_per_chart(bundle):
        query_one, key_one, value_one, valid_one, log_one, delta_one, grad_one = bundle
        key_split = key_one.reshape(back_piece_len, HEADS, head_dim)
        value_split = value_one.reshape(back_piece_len, HEADS, head_dim)
        grad_scores, probs_low = score_grads(
            query_one, key_split, value_split, valid_one, log_one, delta_one, grad_one
        )
        grad_query = (
            jnp.einsum("hqk,khd->hqd", grad_scores, key_split, preferred_element_type=jnp.float32)
            * score_scale
        )
        grad_key = (
            jnp.einsum("hqk,qhd->khd", grad_scores, query_one, preferred_element_type=jnp.float32)
            * score_scale
        )
        grad_value = jnp.einsum(
            "hqk,qhd->khd", probs_low, grad_one, preferred_element_type=jnp.float32
        )
        joined = jnp.concatenate(
            [
                grad_key.reshape(back_piece_len, model_width),
                grad_value.reshape(back_piece_len, model_width),
            ],
            axis=-1,
        )
        return (grad_query, joined)

    query_part, key_part = lax.map(
        back_per_chart,
        (query_heads, key_piece, value_piece, key_valid, log_total, delta, grad_heads),
    )
    key_grads = key_part
    grad_query_acc, key_grads = (query_part, key_grads)
    key_sums = lax.psum_scatter(
        key_grads.astype(jnp.bfloat16), "seq", scatter_dimension=1, tiled=True
    ).astype(jnp.float32)
    grad_key = key_sums[:, :, :model_width].reshape(row_total, model_width).astype(jnp.bfloat16)
    grad_value = key_sums[:, :, model_width:].reshape(row_total, model_width).astype(jnp.bfloat16)
    grad_query = (
        jnp.transpose(grad_query_acc, (0, 2, 1, 3))
        .reshape(row_total, model_width)
        .astype(jnp.bfloat16)
    )
    grad_w_query = jnp.dot(first_in.T, grad_query, preferred_element_type=jnp.float32)
    grad_w_key = jnp.dot(first_in.T, grad_key, preferred_element_type=jnp.float32)
    grad_w_value = jnp.dot(first_in.T, grad_value, preferred_element_type=jnp.float32)
    grad_first = (
        jnp.dot(grad_query, w_query.T, preferred_element_type=jnp.float32)
        + jnp.dot(grad_key, w_key.T, preferred_element_type=jnp.float32)
        + jnp.dot(grad_value, w_value.T, preferred_element_type=jnp.float32)
    )
    _, norm_back_one = jax.vjp(rms_scale, resid_in, gain_one)
    grad_resid_norm, grad_gain_one = norm_back_one(grad_first)
    grad_input = (
        (grad_mid + grad_resid_norm).astype(jnp.bfloat16).reshape(charts, block_len, model_width)
    )
    all_total = lax.psum(
        (
            grad_w_query,
            grad_w_key,
            grad_w_value,
            grad_w_out,
            grad_gain_one,
            grad_w_gate,
            grad_w_up,
            grad_w_down,
            grad_gain_two,
            squares,
            valid_count,
        ),
        ("img", "seq"),
    )
    sum_query, sum_key, sum_value, sum_out, sum_gain_one = (
        all_total[0],
        all_total[1],
        all_total[2],
        all_total[3],
        all_total[4],
    )
    sum_gate, sum_up, sum_down, sum_gain_two = (
        all_total[5],
        all_total[6],
        all_total[7],
        all_total[8],
    )
    sum_squares, sum_count = (all_total[9], all_total[10])
    rms_stats = jnp.sqrt(sum_squares / (sum_count * model_width))
    layer_out = result.astype(jnp.bfloat16).reshape(charts, block_len, model_width)
    return (
        layer_out,
        grad_input,
        sum_gain_one,
        sum_query,
        sum_key,
        sum_value,
        sum_out,
        sum_gain_two,
        sum_gate,
        sum_up,
        sum_down,
        rms_stats,
    )


def solution(mesh):
    return jax.shard_map(
        body,
        mesh=mesh,
        in_specs=(
            P("img", "seq", None),
            P("img"),
            P(),
            P(),
            P(),
            P(),
            P(),
            P(),
            P(),
            P(),
            P(),
            P("img", "seq", None),
        ),
        out_specs=(
            P("img", "seq", None),
            P("img", "seq", None),
            P(),
            P(),
            P(),
            P(),
            P(),
            P(),
            P(),
            P(),
            P(),
            P(),
        ),
        check_vma=False,
    )
```

profile of v0, /device:TPU:0, one launch (start us, length us, event | category | flops | bytes accessed | tf_op | source)
XLA Modules:
  0.0 1047.6 jit_solution(2757531844181256785)
XLA Ops:
  16.0 3.4 convolution_convert_fusion.1
  22.3 3.4 convolution_convert_fusion.3
  25.8 4.2 reshape.241
  29.9 4.3 copy.49
  34.4 62.6 %all-gather.3.cloned.1.call-done = bf16[5,1024,768]{1,2,0:T(8,128)(2,1)} async-done(((bf16[5,128,768]{1,2,0:T(8,128)(2,1)}), bf16[5,1024,768]{1,2,0:T(8,128)(2,1)}) %all-gather.3.cloned.1.call-update) | async-done | bytes 7864336 | tf_op jit(solution)/shard_map/all_gather | solution.py:80
  97.0 78.6 %all-gather.5.cloned.1.call-done = bf16[5,1024,768]{1,2,0:T(8,128)(2,1)} async-done(((bf16[5,128,768]{1,2,0:T(8,128)(2,1)}), bf16[5,1024,768]{1,2,0:T(8,128)(2,1)}) %all-gather.5.cloned.1.call-update) | async-done | bytes 7864336 | tf_op jit(solution)/shard_map/all_gather | solution.py:81
  175.5 95.3 %while.26 = (s32[]{:T(128)}, f32[5,12,128]{2,1,0:T(8,128)}, f32[5,12,128]{2,1,0:T(8,128)}, f32[5,12,128,64]{2,0,3,1:T(8,128)}, pred[5,1024]{1,0:T(8,128)(4,1)S(1...) while((s32[]{:T(128)}, f32[5,12,128]{2,1,0:T(8,128)}, ...), condition=%wide.region_4.5_spmd, body=%wide.region_1.4_spmd.sunk | while | flops 420060672 | bytes 29770880 | solution.py:106
  183.6 11.0 %dynamic_update_slice.27 = f32[5,12,128,64]{2,0,3,1:T(8,128)} dynamic-update-slice(f32[5,12,128,64]{2,0,3,1:T(8,128)} %get-tuple-element.398, f32[1,12,128,64]{2,0,3,1:T(1,128)S(1)} %bitcast.240, s32[]{:T(128)S(6)} %copy.118, s32[]{:T(128)} %constant.82.clone.1..sunk, s32[]{:T(128)} %constant.82.clone.1..sunk, s32[]{:T(128)} %constant.82.clone.1..sunk) | dynamic-update-slice | bytes 786436 | tf_op jit(solution)/shard_map/while/body/jit(dynamic_update_index_in_dim)/dynamic_update_slice | solution.py:106
  202.7 11.0 %dynamic_update_slice.27 = f32[5,12,128,64]{2,0,3,1:T(8,128)} dynamic-update-slice(f32[5,12,128,64]{2,0,3,1:T(8,128)} %get-tuple-element.398, f32[1,12,128,64]{2,0,3,1:T(1,128)S(1)} %bitcast.240, s32[]{:T(128)S(6)} %copy.118, s32[]{:T(128)} %constant.82.clone.1..sunk, s32[]{:T(128)} %constant.82.clone.1..sunk, s32[]{:T(128)} %constant.82.clone.1..sunk) | dynamic-update-slice | bytes 786436 | tf_op jit(solution)/shard_map/while/body/jit(dynamic_update_index_in_dim)/dynamic_update_slice | solution.py:106
  221.8 11.0 %dynamic_update_slice.27 = f32[5,12,128,64]{2,0,3,1:T(8,128)} dynamic-update-slice(f32[5,12,128,64]{2,0,3,1:T(8,128)} %get-tuple-element.398, f32[1,12,128,64]{2,0,3,1:T(1,128)S(1)} %bitcast.240, s32[]{:T(128)S(6)} %copy.118, s32[]{:T(128)} %constant.82.clone.1..sunk, s32[]{:T(128)} %constant.82.clone.1..sunk, s32[]{:T(128)} %constant.82.clone.1..sunk) | dynamic-update-slice | bytes 786436 | tf_op jit(solution)/shard_map/while/body/jit(dynamic_update_index_in_dim)/dynamic_update_slice | solution.py:106
  240.8 11.0 %dynamic_update_slice.27 = f32[5,12,128,64]{2,0,3,1:T(8,128)} dynamic-update-slice(f32[5,12,128,64]{2,0,3,1:T(8,128)} %get-tuple-element.398, f32[1,12,128,64]{2,0,3,1:T(1,128)S(1)} %bitcast.240, s32[]{:T(128)S(6)} %copy.118, s32[]{:T(128)} %constant.82.clone.1..sunk, s32[]{:T(128)} %constant.82.clone.1..sunk, s32[]{:T(128)} %constant.82.clone.1..sunk) | dynamic-update-slice | bytes 786436 | tf_op jit(solution)/shard_map/while/body/jit(dynamic_update_index_in_dim)/dynamic_update_slice | solution.py:106
  259.9 11.0 %dynamic_update_slice.27 = f32[5,12,128,64]{2,0,3,1:T(8,128)} dynamic-update-slice(f32[5,12,128,64]{2,0,3,1:T(8,128)} %get-tuple-element.398, f32[1,12,128,64]{2,0,3,1:T(1,128)S(1)} %bitcast.240, s32[]{:T(128)S(6)} %copy.118, s32[]{:T(128)} %constant.82.clone.1..sunk, s32[]{:T(128)} %constant.82.clone.1..sunk, s32[]{:T(128)} %constant.82.clone.1..sunk) | dynamic-update-slice | bytes 786436 | tf_op jit(solution)/shard_map/while/body/jit(dynamic_update_index_in_dim)/dynamic_update_slice | solution.py:106
  278.8 4.6 fusion.90
  283.4 8.0 multiply_convert_fusion.1
  295.9 3.6 multiply_reduce_fusion.1
  305.7 2.8 copy.54
  311.7 103.4 %while.27 = (s32[]{:T(128)}, bf16[5,12,128,64]{2,3,1,0:T(8,128)(2,1)}, bf16[5,1024,1536]{2,1,0:T(8,128)(2,1)}, pred[5,1024]{1,0:T(8,128)(4,1)S(1)}, bf16[5,128,1...) while((s32[]{:T(128)}, ...), condition=%wide.region_9.10_spmd, body=%wide.region_8.9_spmd.sunk | while | flops 1030324224 | bytes 62580892 | solution.py:195
  316.1 3.3 multiply_convert_fusion.5
  321.4 2.6 fusion.178
  327.5 3.2 copy.108
  336.7 3.3 multiply_convert_fusion.5
  342.0 2.6 fusion.178
  348.1 3.2 copy.108
  357.4 3.3 multiply_convert_fusion.5
  362.6 2.6 fusion.178
  368.7 3.2 copy.108
  378.0 3.3 multiply_convert_fusion.5
  383.3 2.6 fusion.178
  389.4 3.2 copy.108
  398.7 3.3 multiply_convert_fusion.5
  404.0 2.6 fusion.178
  410.0 3.2 copy.108
  417.8 2.5 fusion.61
  424.1 4.8 fusion.93
  428.9 4.6 fusion.94
  433.4 4.6 fusion.95
  438.0 134.3 %reduce-scatter.2.cloned.1.call-done = bf16[5,128,1536]{2,1,0:T(8,128)(2,1)} async-done(((bf16[5,1024,1536]{2,1,0:T(8,128)(2,1)}), bf16[5,128,1536]{2,1,0:T(8,128)(2,1)}) %reduce-scatter.2.cloned.1.call-update) | async-done | bytes 1966096 | tf_op jit(solution)/shard_map/reduce_scatter | solution.py:201
  576.7 2.5 convolution_bitcast_fusion
  580.7 2.7 pad_maximum_fusion
  583.3 3.7 fusion.63
  588.6 2.8 fusion.56
  591.4 39.8 %all-reduce = (f32[768]{0:T(1024)}, f32[768]{0:T(1024)}, f32[4]{0:T(128)S(1)}, f32[]{:T(128)}) all-reduce(f32[768]{0:T(1024)S(1)} %get-tuple-element.170, f32[768]{0:T(1024)S(1)} %get-tuple-element.175, f32[4]{0:T(128)S(1)} %pad_maximum_fusion, f32[]{:T(128)} %get-tuple-element.176), channel_id=1, replica_groups=mesh['img'=4,'seq'=8] {'img','seq'}, use_global_device_ids=true, to_apply=%region_13.14 | all-reduce | flops 1541 | bytes 12328 | tf_op jit(solution)/shard_map/psum | solution.py:224
  632.4 3.4 fusion.52
  635.8 383.2 %all-reduce.4.cloned.1.call-done = (f32[768,768]{1,0:T(8,128)}, f32[768,768]{1,0:T(8,128)}, f32[768,768]{1,0:T(8,128)}, f32[768,768]{1,0:T(8,128)}, f32[768,2048...) async-done(((f32[768,768]{1,0:T(8,128)}, f32[768,768]{1,0:T(8,128)}, f32[768,768]{1,0:T(8,128)}, f32[768,768]{1,0:T(8,128)}, f32[768,2048]{1,0:T(8,128)}, ...) | async-done | bytes 28311568 | tf_op jit(solution)/shard_map/psum | solution.py:224
  1019.0 3.4 copy.144
  1028.4 3.2 copy.148
  1033.0 2.9 copy.149
  1036.6 3.2 copy.150
  (240 shorter events, 154.7 us)
Async XLA Ops:
  7.2 276.2 %copy-start = (bf16[2048,768]{1,0:T(8,128)(2,1)S(1)}, bf16[2048,768]{1,0:T(8,128)(2,1)}, u32[]{:S(2)}) copy-start(bf16[2048,768]{1,0:T(8,128)(2,1)} %param.26) | copy-start | bytes 9437188
  7.2 89.8 %all-gather.3.cloned.1.call-start = ((), (), s32[]{:S(2)}) async-start(), calls=%async_computation.1 | async-start | bytes 8847360 | tf_op jit(solution)/shard_map/all_gather | solution.py:80
  7.2 4.5 copy-start.43
  8.1 5.6 copy-start.30
  10.3 3.4 copy-start.32
  11.8 1.9 copy-start.25
  16.0 159.6 %all-gather.5.cloned.1.call-start = ((), (), s32[]{:S(2)}) async-start(), calls=%async_computation.2 | async-start | bytes 8847360 | tf_op jit(solution)/shard_map/all_gather | solution.py:81
  21.7 550.7 %reduce-scatter.2.cloned.1.call-start = ((), (), s32[]{:S(2)}) async-start(), calls=%async_computation.3 | async-start | bytes 17694720 | tf_op jit(solution)/shard_map/reduce_scatter | solution.py:201
  29.9 4.3 copy-start.39
  29.9 4.3 copy-start.36
  270.8 3.2 copy-start.2
  270.8 3.2 copy-start.42
  274.0 1.9 copy-start.9
  274.1 2.5 copy-start.40
  276.5 2.2 copy-start.7
  276.5 2.2 copy-start.41
  278.8 4.6 copy-start.22
  291.3 2.3 copy-start.15
  291.3 2.3 copy-start.13
  291.3 4.6 copy-start.45
  300.1 3.5 copy-start.4
  305.7 2.8 copy-start.6
  415.1 1.7 copy-start.24
  415.1 603.9 %all-reduce.4.cloned.1.call-start = ((), (), s32[]{:S(2)}) async-start(), calls=%async_computation.4 | async-start | bytes 56623104 | tf_op jit(solution)/shard_map/psum | solution.py:224
  417.6 2.7 copy-start.20
  417.6 2.7 copy-start.5
  417.6 4.0 copy-start.10
  421.6 2.5 copy-start.8
  421.6 2.5 copy-start.16
  424.1 4.8 copy-start.14
  428.9 4.6 copy-start.23
  428.9 4.6 copy-start.46
  572.4 1.8 copy-start.27
  574.1 2.6 copy-start.28
  574.1 2.6 copy-start.11
  583.3 3.8 copy-start.29
  583.3 3.8 copy-start.44
  587.1 1.6 copy-start.21
  1019.0 3.4 copy-start.19
  1019.0 4.8 copy-start.18
  1022.4 6.0 slice-start.4
  1023.8 3.2 copy-start.17
  1023.8 4.6 slice-start.5
  1026.9 4.7 slice-start.2
  1028.4 4.6 slice-start.3
  1028.4 7.5 slice-start
  1033.0 3.6 slice-start.1
  1036.6 4.2 copy-start.1
  (9 other events, 9.2 us)
Sparse Core Ops, SparseCore 0:
  16.1 80.8 all-gather.2
  99.1 76.3 all-gather.4
  415.2 157.0 reduce-scatter.1
  579.8 439.1 all-reduce.3
where the time goes:
time: 1050 us
  waiting for transfers between devices  659 us (63%)
  local copies, waits for them, and re-layouts  151 us (14%)
  matrix products  142 us (14%)
  blocking collectives  39.8 us (4%)
  other arithmetic  39.6 us (4%)
  between operations  15.2 us (1%)
    psum x1, waiting for transfers between devices, body(): lax.psum((grad_w_query, grad_w_key, grad_w_value, grad_w_out, grad_gain_o...  383 us
    reduce_scatter x1, waiting for transfers between devices, body(): lax.psum_scatter(key_grads.astype(jnp.bfloat16), 'seq', scatter_dimension...  134 us
    all_gather x1, waiting for transfers between devices, body(): value_piece = lax.all_gather(value_blocks, 'seq', axis=1, tiled=True)  78.6 us
    all_gather x1, waiting for transfers between devices, body(): key_piece = lax.all_gather(key_blocks, 'seq', axis=1, tiled=True)  62.6 us
    dynamic_update_slice x5, local copies, waits for them, and re-layouts, body(): lax.map(attend_per_chart, (start_state[0], start_state[1], start_state[2]...  54.8 us
    psum x1, blocking collectives, body(): lax.psum((grad_w_query, grad_w_key, grad_w_value, grad_w_out, grad_gain_o...  39.8 us
    unnamed x113, local copies, waits for them, and re-layouts  26.1 us
    dynamic_update_slice x10, local copies, waits for them, and re-layouts, body(): lax.map(back_per_chart, (query_heads, key_piece, value_piece, key_valid,...  25.2 us
  transfers between devices with their start and end apart: 4, of which 4 were waited for; matrix products, arithmetic and copies ran while one was open for 5% of the time, Pallas kernels for 0%

commit v1 on v0

v1 whole, which is shorter than its diff:
```python
import functools
import math

import jax
import jax.numpy as jnp
from jax import lax
from jax.experimental import pallas as pl
from jax.experimental.pallas import tpu as pltpu
from jax.sharding import PartitionSpec as P

HEADS = 12
GROUPS = 4
EPS = 1e-06
NEG = -1000000000.0
LOG2E = 1.4426950408889634
LN2 = 0.6931471805599453
BF = jnp.bfloat16
F32 = jnp.float32
VMEM_LIMIT = 56 * 1024 * 1024


def dot(left, right):
    return jnp.dot(left, right, preferred_element_type=F32)


def dot_nt(left, right):
    return lax.dot_general(left, right, (((1,), (1,)), ((), ())), preferred_element_type=F32)


def dot_tn(left, right):
    return lax.dot_general(left, right, (((0,), (0,)), ((), ())), preferred_element_type=F32)


def split_three(column):
    hi = column.astype(BF).astype(F32)
    rest = column - hi
    mid = rest.astype(BF).astype(F32)
    return hi, mid, rest - mid


def with_extras(values, half, extras):
    lane = lax.broadcasted_iota(jnp.int32, values.shape, 1)
    mine = (lane < 64) if half == 0 else (lane >= 64)
    base = 64 if half == 0 else 0
    out = jnp.where(mine, values, 0.0)
    for offset, column in enumerate(extras):
        if column is not None:
            out = jnp.where(lane == base + offset, column, out)
    return out.astype(BF)


def attend_kernel(q_rows, place_ref, fiq_ref, fik_ref, wq_ref, wk_ref, wv_ref, bias_ref,
                  qx_ref, kx_ref, vx_ref, out_ref):
    del place_ref
    scale = LOG2E / math.sqrt(64.0)
    bias = bias_ref[...]
    key_rows = dot(fik_ref[...], wk_ref[...]).astype(BF).astype(F32)
    value_rows = dot(fik_ref[...], wv_ref[...]).astype(BF).astype(F32)
    for half in range(2):
        kx_ref[half] = with_extras(key_rows, half, (1.0, 1.0, 1.0, bias))
        vx_ref[half] = with_extras(value_rows, half, (1.0, 1.0, 1.0))
    total = fiq_ref.shape[0]
    for start in range(0, total, q_rows):
        rows = pl.ds(start, q_rows)
        query = dot(fiq_ref[rows, :], wq_ref[...]) * scale
        results = []
        for half in range(2):
            base = 64 if half == 0 else 0
            plain = with_extras(query, half, (None, None, None, 1.0))
            scores = dot_nt(plain, kx_ref[half])
            top = jnp.max(scores, axis=1, keepdims=True)
            weights = jnp.exp2(scores - top).astype(BF)
            mixed = dot(weights, vx_ref[half])
            norm = mixed[:, base:base + 1]
            log_total = top + jnp.log2(norm)
            hi, mid, low = split_three(-log_total)
            qx_ref[half, rows, :] = with_extras(query, half, (hi, mid, low, 1.0))
            results.append(mixed / norm)
        lane = lax.broadcasted_iota(jnp.int32, results[0].shape, 1)
        out_ref[rows, :] = jnp.where(lane < 64, results[0], results[1]).astype(BF)


def attend(place, fi_q, fi_k, w_query, w_key, w_value, bias, pairs, q_rows):
    q_total, width = fi_q.shape
    k_total = fi_k.shape[0]
    column = lambda i, place_ref: (0, place_ref[0] * pairs + i)
    whole = lambda i, place_ref: (0, 0)
    stacked = lambda i, place_ref: (i, 0, 0)
    return pl.pallas_call(
        functools.partial(attend_kernel, q_rows),
        grid_spec=pltpu.PrefetchScalarGridSpec(
            num_scalar_prefetch=1,
            grid=(pairs,),
            in_specs=[
                pl.BlockSpec((q_total, width), whole),
                pl.BlockSpec((k_total, width), whole),
                pl.BlockSpec((width, 128), column),
                pl.BlockSpec((width, 128), column),
                pl.BlockSpec((width, 128), column),
                pl.BlockSpec((k_total, 1), whole),
            ],
            out_specs=[
                pl.BlockSpec((2, q_total, 128), stacked),
                pl.BlockSpec((2, k_total, 128), stacked),
                pl.BlockSpec((2, k_total, 128), stacked),
                pl.BlockSpec((q_total, 128), lambda i, place_ref: (0, i)),
            ],
        ),
        out_shape=[
            jax.ShapeDtypeStruct((2 * pairs, q_total, 128), BF),
            jax.ShapeDtypeStruct((2 * pairs, k_total, 128), BF),
            jax.ShapeDtypeStruct((2 * pairs, k_total, 128), BF),
            jax.ShapeDtypeStruct((q_total, pairs * 128), BF),
        ],
        compiler_params=pltpu.CompilerParams(vmem_limit_bytes=VMEM_LIMIT),
        cost_estimate=pl.CostEstimate(
            flops=2 * 128 * pairs * (2 * q_total * k_total + width * (q_total + 2 * k_total)),
            bytes_accessed=2 * (q_total + k_total) * width * 4,
            transcendentals=2 * pairs * q_total * k_total,
        ),
    )(place, fi_q, fi_k, w_query, w_key, w_value, bias)


def attend_back_kernel(q_rows, qx_ref, kx_ref, vx_ref, out_ref, grad_ref, dq_ref, dk_ref, dv_ref):
    q_total, k_total = qx_ref.shape[1], kx_ref.shape[1]
    dk_all, dv_all = [], []
    lane_k = lax.broadcasted_iota(jnp.int32, (k_total, 128), 1)
    keys_pair = jnp.where(lane_k < 64, kx_ref[0], kx_ref[1])
    keys_trans = jnp.transpose(keys_pair.astype(F32)).astype(BF)
    dq_trans = [[], []]
    for half in range(2):
        dk_sum = jnp.zeros((k_total, 128), F32)
        dv_sum = jnp.zeros((k_total, 128), F32)
        for start in range(0, q_total, q_rows):
            rows = pl.ds(start, q_rows)
            grad = grad_ref[rows, :].astype(F32)
            lane = lax.broadcasted_iota(jnp.int32, grad.shape, 1)
            mine = (lane < 64) if half == 0 else (lane >= 64)
            delta = jnp.sum(jnp.where(mine, grad * out_ref[rows, :].astype(F32), 0.0), axis=1, keepdims=True)
            hi, mid, low = split_three(-delta)
            grad_x = with_extras(grad, half, (hi, mid, low))
            query_x = qx_ref[half, rows, :]
            probs = jnp.exp2(dot_nt(kx_ref[half], query_x))
            centred = dot_nt(vx_ref[half], grad_x)
            grad_scores = (probs * centred).astype(BF)
            dv_sum = dv_sum + dot(probs.astype(BF), grad_x)
            dk_sum = dk_sum + dot(grad_scores, query_x)
            dq_trans[half].append(dot(keys_trans[64 * half:64 * half + 64, :], grad_scores))
        dk_all.append(dk_sum)
        dv_all.append(dv_sum)
    for index, start in enumerate(range(0, q_total, q_rows)):
        joined = jnp.concatenate([dq_trans[0][index], dq_trans[1][index]], axis=0)
        dq_ref[pl.ds(start, q_rows), :] = (jnp.transpose(joined) * 0.125).astype(BF)
    dk_ref[...] = (jnp.where(lane_k < 64, dk_all[0], dk_all[1]) * LN2).astype(BF)
    dv_ref[...] = jnp.where(lane_k < 64, dv_all[0], dv_all[1]).astype(BF)


def attend_back(qx, kx, vx, out, grad, q_rows):
    heads, q_total, _ = qx.shape
    k_total = kx.shape[1]
    pairs = heads // 2
    stacked = lambda i: (i, 0, 0)
    flat = lambda i: (0, i)
    return pl.pallas_call(
        functools.partial(attend_back_kernel, q_rows),
        grid=(pairs,),
        in_specs=[
            pl.BlockSpec((2, q_total, 128), stacked),
            pl.BlockSpec((2, k_total, 128), stacked),
            pl.BlockSpec((2, k_total, 128), stacked),
            pl.BlockSpec((q_total, 128), flat),
            pl.BlockSpec((q_total, 128), flat),
        ],
        out_specs=[
            pl.BlockSpec((q_total, 128), flat),
            pl.BlockSpec((k_total, 128), flat),
            pl.BlockSpec((k_total, 128), flat),
        ],
        out_shape=[
            jax.ShapeDtypeStruct((q_total, pairs * 128), BF),
            jax.ShapeDtypeStruct((k_total, pairs * 128), BF),
            jax.ShapeDtypeStruct((k_total, pairs * 128), BF),
        ],
        compiler_params=pltpu.CompilerParams(vmem_limit_bytes=VMEM_LIMIT),
        cost_estimate=pl.CostEstimate(
            flops=2 * 128 * pairs * 5 * q_total * k_total,
            bytes_accessed=2 * 128 * heads * (q_total + 2 * k_total),
            transcendentals=heads * q_total * k_total,
        ),
    )(qx, kx, vx, out, grad)


def norm_scale(values):
    return lax.rsqrt(jnp.mean(values * values, axis=-1, keepdims=True) + EPS)


def norm_back(values, gain, grad):
    scale = norm_scale(values)
    scaled = values * scale
    weighted = grad * gain
    inner = jnp.mean(weighted * scaled, axis=-1, keepdims=True)
    return scale * (weighted - scaled * inner), jnp.sum(grad * scaled, axis=0)


def mlp_core(gate_in, up_in):
    return jax.nn.gelu(gate_in, approximate=True) * up_in


def masked_squares(values_in, row_mask):
    return jnp.sum(row_mask * jnp.sum(values_in * values_in, axis=-1))


def body(n_img, n_seq, patches, counts, norm_gain_one, w_query, w_key, w_value, w_out,
         norm_gain_two, w_gate, w_up, w_down, cotangent):
    charts, block_len, width = patches.shape
    members = n_seq // GROUPS
    head_count = HEADS // members
    pairs = -(-head_count // 2)
    pad_cols = pairs * 128 - head_count * 64
    mine_cols = head_count * 64
    main_own = GROUPS * block_len
    seq_len = n_seq * block_len
    here = lax.axis_index("seq")
    group, member = here // members, here % members

    def shift_perm(step):
        return [(g * members + r, ((g + step) % GROUPS) * members + r)
                for g in range(GROUPS) for r in range(members)]

    def member_perm(step):
        return [(g * members + r, g * members + (r ^ step))
                for g in range(GROUPS) for r in range(members)]

    def to_groups(array):
        pieces = []
        for step in range(GROUPS):
            part = lax.dynamic_index_in_dim(array, (group + step) % GROUPS, 0, keepdims=False)
            pieces.append(part if step == 0 else lax.ppermute(part, "seq", shift_perm(step)))
        return pieces

    def from_groups(rows):
        pieces = []
        for step in range(GROUPS):
            part = rows[step * block_len:(step + 1) * block_len]
            pieces.append(part if step == 0 else lax.ppermute(part, "seq", shift_perm(-step)))
        ring = jnp.stack(pieces + pieces)
        return lax.dynamic_slice_in_dim(ring, (GROUPS - group) % GROUPS, GROUPS, 0)

    def to_members(own):
        return [own] + [lax.ppermute(own, "seq", member_perm(step)) for step in range(1, members)]

    def columns_of(weight, who):
        part = lax.dynamic_slice_in_dim(weight, who * mine_cols, mine_cols, 1)
        return jnp.pad(part, ((0, 0), (0, pad_cols))) if pad_cols else part

    gain_one = norm_gain_one.astype(F32)
    gain_two = norm_gain_two.astype(F32)
    steps = jnp.arange(GROUPS, dtype=jnp.int32)
    block_of = ((group - steps) % GROUPS) * members
    inside = jnp.arange(block_len, dtype=jnp.int32)

    def main_positions(who):
        return ((block_of + who) * block_len)[:, None] + inside[None, :]

    count_main = lax.dynamic_index_in_dim(counts, group, 0, keepdims=False)
    count_rest = counts[GROUPS]
    rest_positions = here * block_len + inside
    row_valid = jnp.concatenate([
        (main_positions(member) < count_main).reshape(-1), rest_positions < count_rest])
    row_mask = row_valid.astype(F32)
    key_positions = jnp.concatenate(
        [main_positions(member ^ step).reshape(-1) for step in range(members)])
    bias_main = jnp.where(key_positions < count_main, 0.0, NEG).astype(F32)[:, None]
    bias_rest = jnp.where(jnp.arange(seq_len) < count_rest, 0.0, NEG).astype(F32)[:, None]

    rest_rows = patches[GROUPS]
    rest_f32 = rest_rows.astype(F32)
    first_rest = (rest_f32 * norm_scale(rest_f32) * gain_one).astype(BF)
    moved = to_groups(patches)
    first_rest_all = lax.all_gather(first_rest, "seq", axis=0, tiled=True)
    main_rows = jnp.concatenate(moved, axis=0).astype(F32)
    first_main = (main_rows * norm_scale(main_rows) * gain_one).astype(BF)
    first_all = jnp.concatenate(to_members(first_main), axis=0)
    grad_moved = to_groups(cotangent)

    place = jnp.reshape(member, (1,)).astype(jnp.int32)
    zero_place = jnp.zeros((1,), jnp.int32)
    if pad_cols:
        main_weights = [columns_of(w, member) for w in (w_query, w_key, w_value)]
        main_place = zero_place
    else:
        main_weights = [w_query, w_key, w_value]
        main_place = place
    q_rows = 256
    qx_main, kx_main, vx_main, attn_main = attend(
        main_place, first_all, first_all, *main_weights, bias_main, pairs, q_rows)
    qx_rest, kx_rest, vx_rest, attn_rest = attend(
        zero_place, first_rest, first_rest_all, w_query, w_key, w_value, bias_rest,
        HEADS // 2, min(q_rows, block_len))

    def swap_in(array):
        pieces = []
        for step in range(members):
            part = array[step * main_own:(step + 1) * main_own, :mine_cols]
            pieces.append(part if step == 0 else lax.ppermute(part, "seq", member_perm(step)))
        out = jnp.zeros((main_own, width), array.dtype)
        for step in range(members):
            out = lax.dynamic_update_slice_in_dim(out, pieces[step], (member ^ step) * mine_cols, 1)
        return out

    attn_in = jnp.concatenate([swap_in(attn_main), attn_rest], axis=0)
    resid = jnp.concatenate([main_rows, rest_f32], axis=0)
    branch_one = dot(attn_in, w_out)
    middle = resid + branch_one
    second_in = (middle * norm_scale(middle) * gain_two).astype(BF)
    gate_rows = dot(second_in, w_gate)
    up_rows = dot(second_in, w_up)
    inner = mlp_core(gate_rows, up_rows).astype(BF)
    branch_two = dot(inner, w_down)
    result = middle + branch_two
    squares = jnp.stack([masked_squares(v, row_mask) for v in (resid, branch_one, branch_two, result)])
    valid_count = jnp.sum(row_mask)
    result_low = result.astype(BF)
    layer_out = jnp.concatenate(
        [from_groups(result_low[:main_own]), result_low[main_own:][None]], axis=0)

    grad_low = jnp.concatenate(grad_moved + [cotangent[GROUPS]], axis=0)
    grad_out = grad_low.astype(F32)

    def total(*arrays):
        return lax.psum(tuple(a.astype(BF) for a in arrays), ("img", "seq"))

    (sum_down,) = total(dot_tn(inner, grad_low))
    grad_inner = dot_nt(grad_low, w_down)
    _, mlp_back = jax.vjp(mlp_core, gate_rows, up_rows)
    grad_gate, grad_up = mlp_back(grad_inner)
    grad_gate = grad_gate.astype(BF)
    grad_up = grad_up.astype(BF)
    sum_gate, sum_up = total(dot_tn(second_in, grad_gate), dot_tn(second_in, grad_up))
    grad_second = dot_nt(grad_gate, w_gate) + dot_nt(grad_up, w_up)
    grad_mid_norm, grad_gain_two = norm_back(middle, gain_two, grad_second)
    grad_mid = grad_out + grad_mid_norm
    grad_mid_low = grad_mid.astype(BF)
    part_out = dot_tn(attn_in, grad_mid_low)

    main_grads = []
    for step in range(members):
        rows_of = lax.dynamic_slice_in_dim(w_out, (member ^ step) * mine_cols, mine_cols, 0)
        part = dot_nt(grad_mid_low[:main_own], rows_of).astype(BF)
        if pad_cols:
            part = jnp.pad(part, ((0, 0), (0, pad_cols)))
        main_grads.append(part if step == 0 else lax.ppermute(part, "seq", member_perm(step)))
    grad_attn_main = jnp.concatenate(main_grads, axis=0)
    grad_attn_rest = dot_nt(grad_mid_low[main_own:], w_out).astype(BF)

    dq_rest, dk_rest, dv_rest = attend_back(
        qx_rest, kx_rest, vx_rest, attn_rest, grad_attn_rest, min(q_rows, block_len))
    first_part_rest = (dot_nt(dk_rest, w_key) + dot_nt(dv_rest, w_value)).astype(BF)
    first_sum_rest = lax.psum_scatter(first_part_rest, "seq", scatter_dimension=0, tiled=True)
    dq_main, dk_main, dv_main = attend_back(
        qx_main, kx_main, vx_main, attn_main, grad_attn_main, q_rows)

    main_parts = [(dq_main, w_query), (dk_main, w_key), (dv_main, w_value)]
    first_part_main = sum(
        dot_nt(part[:, :mine_cols], lax.dynamic_slice_in_dim(w, member * mine_cols, mine_cols, 1))
        for part, w in main_parts)
    grad_first_main = first_part_main[:main_own]
    for step in range(1, members):
        part = first_part_main[step * main_own:(step + 1) * main_own].astype(BF)
        grad_first_main = grad_first_main + lax.ppermute(part, "seq", member_perm(step)).astype(F32)
    grad_first_rest = dot_nt(dq_rest, w_query) + first_sum_rest.astype(F32)
    grad_first = jnp.concatenate([grad_first_main, grad_first_rest], axis=0)

    qkv_parts = []
    rest_parts = [(first_rest, dq_rest), (first_rest_all, dk_rest), (first_rest_all, dv_rest)]
    for (part, _), (fi_rest, part_rest) in zip(main_parts, rest_parts):
        whole = dot_tn(fi_rest, part_rest)
        local = dot_tn(first_all, part[:, :mine_cols])
        spot = lax.dynamic_slice_in_dim(whole, member * mine_cols, mine_cols, 1)
        qkv_parts.append(lax.dynamic_update_slice_in_dim(whole, spot + local, member * mine_cols, 1))
    sum_query, sum_key, sum_value, sum_out = total(*qkv_parts, part_out)

    grad_resid_norm, grad_gain_one = norm_back(resid, gain_one, grad_first)
    grad_input_rows = (grad_mid + grad_resid_norm).astype(BF)
    grad_input = jnp.concatenate(
        [from_groups(grad_input_rows[:main_own]), grad_input_rows[main_own:][None]], axis=0)
    sum_gain_one, sum_gain_two, sum_squares, sum_count = lax.psum(
        (grad_gain_one, grad_gain_two, squares, valid_count), ("img", "seq"))
    rms_stats = jnp.sqrt(sum_squares / (sum_count * width))
    wide = lambda a: a.astype(F32)
    return (layer_out, grad_input, sum_gain_one, wide(sum_query), wide(sum_key), wide(sum_value),
            wide(sum_out), sum_gain_two, wide(sum_gate), wide(sum_up), wide(sum_down), rms_stats)


def solution(mesh):
    rows = P("img", "seq", None)
    return jax.shard_map(
        functools.partial(body, mesh.shape["img"], mesh.shape["seq"]),
        mesh=mesh,
        in_specs=(rows, P("img"), P(), P(), P(), P(), P(), P(), P(), P(), P(), rows),
        out_specs=(rows, rows, P(), P(), P(), P(), P(), P(), P(), P(), P(), P()),
        check_vma=False,
    )
```

time: 1050 us -> 520 us (0.50)
  waiting for transfers between devices: 659 us -> 217 us
  local copies, waits for them, and re-layouts: 151 us -> 29.4 us
  matrix products: 142 us -> 65.1 us
  Pallas kernels: 0 us -> 65 us
  starting transfers between devices: 0.69 us -> 22.5 us
  other arithmetic: 39.6 us -> 53.8 us
    psum x1, waiting for transfers between devices: 383 us -> 197 us  [total(): return lax.psum(tuple((a.astype(BF) for a in arrays)), ('img', 'seq'))]
    all_gather x2 -> x1, waiting for transfers between devices: 141 us -> 0.01 us  [body(): first_rest_all = lax.all_gather(first_rest, 'seq', axis=0, tiled=True)]
    reduce_scatter x1, waiting for transfers between devices: 134 us -> 0.02 us  [body(): lax.psum_scatter(first_part_rest, 'seq', scatter_dimension=0, tiled=True)]
    dynamic_update_slice x15 -> x1, local copies, waits for them, and re-layouts: 80.1 us -> 0.79 us  [swap_in(): lax.dynamic_update_slice_in_dim(out, pieces[step], (member ^ step) * mine...]
    dot_general x56 -> x26, matrix products: 142 us -> 65.1 us  [the longest x12 27.5 us: dot_nt(): lax.dot_general(left, right, (((1,), (1,)), ((), ())), preferred_element_...]
    pallas_call x0 -> x4, Pallas kernels: none -> 65 us  [the longest x2 36.9 us: attend(): pl.pallas_call(functools.partial(attend_kernel, q_rows), grid_spec=pltpu....]
    convert_element_type x7 -> x19, other arithmetic: 8.48 us -> 35.2 us  [the longest x7 18.6 us: body(): wide = lambda a: a.astype(F32)]
    ppermute x0 -> x16, starting transfers between devices: none -> 22.4 us  [the longest x6 10.9 us: from_groups(): lax.ppermute(part, 'seq', shift_perm(-step))]
  transfers between devices with their start and end apart: 4 -> 19, of which waited for: 4 -> 4; matrix products, arithmetic and copies ran while one was open for 5% -> 16% of each run, Pallas kernels for 0% -> 10%
where the time goes in v1:
time: 520 us; the launch traced here: 516 us
  waiting for transfers between devices  217 us (42%)
  matrix products  65.1 us (13%)
  Pallas kernels  65 us (12%)
  other arithmetic  53.8 us (10%)
  blocking collectives  48.2 us (9%)
  local copies, waits for them, and re-layouts  29.4 us (6%)
  starting transfers between devices  22.5 us (4%)
  between operations  15.5 us (3%)
    psum x1, waiting for transfers between devices, total(): return lax.psum(tuple((a.astype(BF) for a in arrays)), ('img', 'seq'))  197 us
    psum x1, blocking collectives, body(): lax.psum((grad_gain_one, grad_gain_two, squares, valid_count), ('img', 's...  48.2 us
    pallas_call x2, Pallas kernels, attend(): pl.pallas_call(functools.partial(attend_kernel, q_rows), grid_spec=pltpu....  36.9 us
    pallas_call x2, Pallas kernels, attend_back(): pl.pallas_call(functools.partial(attend_back_kernel, q_rows), grid=(pairs...  28.1 us
    dot_general x12, matrix products, dot_nt(): lax.dot_general(left, right, (((1,), (1,)), ((), ())), preferred_element_...  27.5 us
    dot_general x10, matrix products, dot_tn(): lax.dot_general(left, right, (((0,), (0,)), ((), ())), preferred_element_...  25.9 us
    ppermute x6, waiting for transfers between devices, to_groups(): lax.ppermute(part, 'seq', shift_perm(step))  19.2 us
    convert_element_type x7, other arithmetic, body(): wide = lambda a: a.astype(F32)  18.6 us
  transfers between devices with their start and end apart: 19, of which 4 were waited for; matrix products, arithmetic and copies ran while one was open for 16% of the time, Pallas kernels for 10%

profile of v1, /device:TPU:0, one launch (start us, length us, event | category | flops | bytes accessed | tf_op | source)
XLA Modules:
  0.0 516.3 jit_solution(2451817338452786522)
XLA Ops:
  7.4 2.3 bitcast_convert_fusion
  9.7 3.0 collective-permute-start
  12.7 2.6 collective-permute-start.1
  17.7 1.7 multiply_convert_fusion.4.fiq_ref
  19.5 1.9 dynamic-slice_bitcast_fusion
  26.1 2.9 collective-permute-start.10
  32.4 1.5 fusion.21.bias_ref
  34.7 1.6 bitcast_dynamic-update-slice_fusion.7
  37.5 1.6 constant_dynamic-update-slice_fusion.2
  39.1 18.8 %collective-permute-done.9 = bf16[128,768]{1,0:T(8,128)(2,1)} collective-permute-done((bf16[128,768]{1,0:T(8,128)(2,1)}, bf16[128,768]{1,0:T(8,128)(2,1)}, u32[]{:S(2)}, u32[]{:S(2)}) %collective-permute-start.9) | collective-permute-done | bytes 196640 | tf_op jit(solution)/shard_map/ppermute | solution.py:238
  58.0 1.6 constant_dynamic-update-slice_fusion.1
  61.7 21.6 %shard_map.211 = (bf16[6,1024,128]{2,1,0:T(8,128)(2,1)}, bf16[6,1024,128]{2,1,0:T(8,128)(2,1)}, bf16[6,1024,128]{2,1,0:T(8,128)(2,1)}, bf16[1024,384]{1,0:T(8,128)(2,1)}) custom-call(s32[1]{0:T(128)} %bitcast.5.place_ref, bf16[1024,768]{1,0:T(8,128)(2,1)} %pad_maximum_fusion.2.fiq_ref.fik_ref, bf16[1024,768]{1,0:T(8,128)(2,1)} %pad_maximum_fusion.2.fiq_ref.fik_ref, ...), custom_call_target="tpu_custom_call" | custom-call | flops 3422552064 | bytes 12582912 | tf_op jit(solution)/shard_map/pallas_call | solution.py:89
  84.3 1.9 fusion.40
  86.9 2.4 maximum_convert_fusion
  89.3 1.6 bitcast_dynamic-update-slice_fusion.6
  91.7 15.3 %shard_map.212 = (bf16[12,128,128]{2,1,0:T(8,128)(2,1)}, bf16[12,1024,128]{2,1,0:T(8,128)(2,1)}, bf16[12,1024,128]{2,1,0:T(8,128)(2,1)}, bf16[128,768]{1,0:T(8,128)(2,1)}) custom-call(s32[1]{0:T(128)} %constant.139.clone.1.place_ref, bf16[128,768]{1,0:T(8,128)(2,1)} %multiply_convert_fusion.4.fiq_ref, ...), custom_call_target="tpu_custom_call" | custom-call | flops 2969567232 | bytes 7077888 | tf_op jit(solution)/shard_map/pallas_call | solution.py:89
  107.0 3.1 multiply_reduce_fusion.8
  110.4 2.2 fusion.42
  113.1 2.2 fusion.43
  115.3 9.2 %multiply_convert_fusion = (bf16[640,2048]{1,0:T(8,128)(2,1)}, bf16[640,2048]{1,0:T(8,128)(2,1)S(1)}, bf16[640,2048]{1,0:T(8,128)(2,1)}) fusion(f32[640,2048]{1,0:T(8,128)S(1)} %fusion.42, f32[640,2048]{1,0:T(8,128)S(1)} %fusion.43, bf16[640,768]{1,0:T(8,128)(2,1)} %bitcast_dynamic-update-slice_fusion.6, bf16[2048,768]{1,0:T(8,128)(2,1)S(1)} %copy-done), kind=kOutput, calls=%fused_computation.9 | convolution fusion | flops 2047344640 | bytes 22478848 | tf_op jit(solution)/shard_map/dot_general | solution.py:27
  124.6 2.2 fusion.44
  127.3 2.2 convolution_add_fusion
  129.5 4.2 multiply_reduce_fusion.1
  133.7 1.8 fusion.36
  138.7 3.3 convolution_convert_fusion.3
  142.0 4.0 convolution_convert_fusion.1
  146.5 8.9 %shard_map.214 = (bf16[128,768]{1,0:T(8,128)(2,1)}, bf16[1024,768]{1,0:T(8,128)(2,1)}, bf16[1024,768]{1,0:T(8,128)(2,1)}) custom-call(bf16[12,128,128]{2,1,0:T(8,128)(2,1)} %get-tuple-element.34.qx_ref, bf16[12,1024,128]{2,1,0:T(8,128)(2,1)} %get-tuple-element.35.kx_ref, bf16[12,1024,128]{2,1,0:T(8,128)(2,1)} %get-tuple-element.36.vx_ref, ...), custom_call_target="tpu_custom_call" | custom-call | flops 1006632960 | bytes 6684672 | tf_op jit(solution)/shard_map/pallas_call | solution.py:164
  155.5 3.0 fusion.45
  158.5 2.6 add_convert_fusion
  163.2 5.8 %collective-permute-start.5 = (bf16[128,768]{1,0:T(8,128)(2,1)}, bf16[128,768]{1,0:T(8,128)(2,1)S(1)}, u32[]{:S(2)}, u32[]{:S(2)}) collective-permute-start(bf16[128,768]{1,0:T(8,128)(2,1)} %get-tuple-element.82), channel_id=1, source_target_pairs={{0,6},{1,7},{2,0},{3,1},{4,2},{5,3},{6,4},{7,5},{8,14},{9,15},{10,... | collective-permute-start | bytes 589832 | tf_op jit(solution)/shard_map/ppermute | solution.py:245
  173.0 4.0 convolution_convert_fusion.2
  177.0 5.4 %convolution_convert_fusion = bf16[2048,768]{1,0:T(8,128)(2,1)} fusion(bf16[640,2048]{1,0:T(8,128)(2,1)S(1)} %copy-done.59, bf16[640,768]{1,0:T(8,128)(2,1)} %bitcast_dynamic-update-slice_fusion.6), kind=kOutput, calls=%fused_computation.12 | convolution fusion | flops 2014838784 | bytes 6750208 | tf_op jit(solution)/shard_map/dot_general | solution.py:31
  182.4 3.1 pad_maximum_fusion.9
  185.5 2.9 fusion.47
  189.3 19.2 %shard_map.213 = (bf16[1024,384]{1,0:T(8,128)(2,1)}, bf16[1024,384]{1,0:T(8,128)(2,1)}, bf16[1024,384]{1,0:T(8,128)(2,1)}) custom-call(bf16[6,1024,128]{2,1,0:T(8,128)(2,1)} %get-tuple-element.28.qx_ref, bf16[6,1024,128]{2,1,0:T(8,128)(2,1)} %get-tuple-element.29.kx_ref, bf16[6,1024,128]{2,1,0:T(8,128)(2,1)} %get-tuple-element.30.vx_ref, ...), custom_call_target="tpu_custom_call" | custom-call | flops 4026531840 | bytes 4718592 | tf_op jit(solution)/shard_map/pallas_call | solution.py:164
  208.5 2.3 fusion.7
  227.2 2.0 convolution_add_fusion.4
  231.4 3.3 add_convert_fusion.1
  236.0 3.5 collective-permute-start.13
  240.6 48.2 %all-reduce = (f32[768]{0:T(1024)}, f32[768]{0:T(1024)}, f32[4]{0:T(128)S(1)}, f32[]{:T(128)}) all-reduce(f32[768]{0:T(1024)} %get-tuple-element.42, f32[768]{0:T(1024)} %get-tuple-element.47, f32[4]{0:T(128)} %pad_maximum_fusion.9, f32[]{:T(128)} %get-tuple-element.48), channel_id=1, replica_groups=mesh['img'=4,'seq'=8] {'img','seq'}, use_global_device_ids=true, to_apply=%region_8.9 | all-reduce | flops 1541 | bytes 12328 | tf_op jit(solution)/shard_map/psum | solution.py:387
  293.1 197.0 %all-reduce.4.cloned.1.call-done = (bf16[768,768]{1,0:T(8,128)(2,1)}, bf16[768,768]{1,0:T(8,128)(2,1)}, bf16[768,768]{1,0:T(8,128)(2,1)}, bf16[768,768]{1,0:T(8,...) async-done(((bf16[768,768]{1,0:T(8,128)(2,1)}, bf16[768,768]{1,0:T(8,128)(2,1)}, bf16[768,768]{1,0:T(8,128)(2,1)}, ...) | async-done | bytes 14155792 | tf_op jit(solution)/shard_map/psum | solution.py:331
  490.1 5.6 %convert_element_type.139 = f32[768,2048]{1,0:T(8,128)} convert(bf16[768,2048]{1,0:T(8,128)(2,1)} %get-tuple-element.61) | non-fusion elementwise | flops 1572864 | bytes 9437184 | tf_op jit(solution)/shard_map/convert_element_type | solution.py:390
  495.7 3.6 convert_element_type.141
  499.2 3.2 convert_element_type.143
  502.4 1.6 convert_element_type.131
  504.1 1.6 convert_element_type.133
  505.7 1.6 convert_element_type.135
  507.4 1.6 convert_element_type.137
  (220 shorter events, 54.1 us)
Async XLA Ops:
  7.2 108.1 %copy-start = (bf16[2048,768]{1,0:T(8,128)(2,1)S(1)}, bf16[2048,768]{1,0:T(8,128)(2,1)}, u32[]{:S(2)}) copy-start(bf16[2048,768]{1,0:T(8,128)(2,1)} %param.22) | copy-start | bytes 9437188
  7.2 10.5 %copy-start.44 = (bf16[768]{0:T(1024)(128)(2,1)S(1)}, bf16[768]{0:T(1024)(128)(2,1)}, u32[]{:S(2)}) copy-start(bf16[768]{0:T(1024)(128)(2,1)} %param.14) | copy-start | bytes 4612
  7.2 84.5 %all-gather.2.cloned.1.call-start = ((), (), s32[]{:S(2)}) async-start(), calls=%async_computation.1 | async-start | bytes 1769472 | tf_op jit(solution)/shard_map/all_gather | solution.py:280
  7.3 15.3 %copy-start.46 = (s32[5]{0:T(128)S(1)}, s32[5]{0:T(128)}, u32[]{:S(2)}) copy-start(s32[5]{0:T(128)} %param.13) | copy-start | bytes 64
  7.4 18.7 %copy-start.45 = (bf16[768]{0:T(1024)(128)(2,1)S(1)}, bf16[768]{0:T(1024)(128)(2,1)}, u32[]{:S(2)}) copy-start(bf16[768]{0:T(1024)(128)(2,1)} %param.19) | copy-start | bytes 4612
  9.7 16.4 %collective-permute-start = (bf16[128,768]{1,0:T(8,128)(2,1)}, bf16[128,768]{1,0:T(8,128)(2,1)}, u32[]{:S(2)}, u32[]{:S(2)}) collective-permute-start(bf16[128,768]{1,0:T(8,128)(2,1)} %get-tuple-element.85), channel_id=1, source_target_pairs={{0,2},{1,3},{2,4},{3,5},{4,6},{5,7},{6,0},{7,1},{8,10},{9,11},{10,... | collective-permute-start | bytes 589832 | tf_op jit(solution)/shard_map/ppermute | solution.py:238
  12.7 16.6 %collective-permute-start.1 = (bf16[128,768]{1,0:T(8,128)(2,1)}, bf16[128,768]{1,0:T(8,128)(2,1)}, u32[]{:S(2)}, u32[]{:S(2)}) collective-permute-start(bf16[128,768]{1,0:T(8,128)(2,1)} %get-tuple-element.84), channel_id=1, source_target_pairs={{0,4},{1,5},{2,6},{3,7},{4,0},{5,1},{6,2},{7,3},{8,12},{9,13},{10,... | collective-permute-start | bytes 589832 | tf_op jit(solution)/shard_map/ppermute | solution.py:238
  15.3 14.1 %collective-permute-start.2 = (bf16[128,768]{1,0:T(8,128)(2,1)}, bf16[128,768]{1,0:T(8,128)(2,1)}, u32[]{:S(2)}, u32[]{:S(2)}) collective-permute-start(bf16[128,768]{1,0:T(8,128)(2,1)} %get-tuple-element.87), channel_id=1, source_target_pairs={{0,6},{1,7},{2,0},{3,1},{4,2},{5,3},{6,4},{7,5},{8,14},{9,15},{10,... | collective-permute-start | bytes 589832 | tf_op jit(solution)/shard_map/ppermute | solution.py:238
  19.5 207.7 %reduce-scatter.2.cloned.1.call-start = ((), (), s32[]{:S(2)}) async-start(), calls=%async_computation.2 | async-start | bytes 1769472 | tf_op jit(solution)/shard_map/reduce_scatter | solution.py:359
  21.5 16.1 %collective-permute-start.8 = (bf16[128,768]{1,0:T(8,128)(2,1)}, bf16[128,768]{1,0:T(8,128)(2,1)}, u32[]{:S(2)}, u32[]{:S(2)}) collective-permute-start(bf16[128,768]{1,0:T(8,128)(2,1)} %get-tuple-element.78), channel_id=1, source_target_pairs={{0,2},{1,3},{2,4},{3,5},{4,6},{5,7},{6,0},{7,1},{8,10},{9,11},{10,... | collective-permute-start | bytes 589832 | tf_op jit(solution)/shard_map/ppermute | solution.py:238
  22.1 35.8 %collective-permute-start.9 = (bf16[128,768]{1,0:T(8,128)(2,1)}, bf16[128,768]{1,0:T(8,128)(2,1)}, u32[]{:S(2)}, u32[]{:S(2)}) collective-permute-start(bf16[128,768]{1,0:T(8,128)(2,1)} %get-tuple-element.77), channel_id=1, source_target_pairs={{0,4},{1,5},{2,6},{3,7},{4,0},{5,1},{6,2},{7,3},{8,12},{9,13},{10,... | collective-permute-start | bytes 589832 | tf_op jit(solution)/shard_map/ppermute | solution.py:238
  26.1 7.8 %copy-start.33 = (pred[1024,1]{1,0:T(8,128)(4,1)S(1)}, pred[1024,1]{1,0:T(8,128)(4,1)}, u32[]{:S(2)}) copy-start(pred[1024,1]{1,0:T(8,128)(4,1)} %copy.28) | copy-start | bytes 3076
  26.1 60.1 %collective-permute-start.10 = (bf16[128,768]{1,0:T(8,128)(2,1)}, bf16[128,768]{1,0:T(8,128)(2,1)S(1)}, u32[]{:S(2)}, u32[]{:S(2)}) collective-permute-start(bf16[128,768]{1,0:T(8,128)(2,1)} %get-tuple-element.76), channel_id=1, source_target_pairs={{0,6},{1,7},{2,0},{3,1},{4,2},{5,3},{6,4},{7,5},{8,14},{9,15},{10,... | collective-permute-start | bytes 589832 | tf_op jit(solution)/shard_map/ppermute | solution.py:238
  32.3 29.4 %copy-start.9 = (bf16[512,768]{1,0:T(8,128)(2,1)}, bf16[512,768]{1,0:T(8,128)(2,1)S(1)}, u32[]{:S(2)}) copy-start(bf16[512,768]{1,0:T(8,128)(2,1)S(1)} %multiply_convert_fusion.3) | copy-start | bytes 2359300
  32.3 27.3 %collective-permute-start.3 = (bf16[512,768]{1,0:T(8,128)(2,1)S(1)}, bf16[512,768]{1,0:T(8,128)(2,1)S(1)}, u32[]{:S(2)}, u32[]{:S(2)}) collective-permute-start(bf16[512,768]{1,0:T(8,128)(2,1)S(1)} %multiply_convert_fusion.3), channel_id=1, source_target_pairs={{0,1},{1,0},{2,3},{3,2},{4,5},{5,4},{6,7},{7,6},{8,9},{9,8},{10,11... | collective-permute-start | bytes 2359304 | tf_op jit(solution)/shard_map/ppermute | solution.py:250
  83.3 3.6 copy-start.8
  86.2 4.7 collective-permute-start.4
  91.7 15.3 %copy-start.4 = (f32[512,768]{1,0:T(8,128)S(1)}, f32[512,768]{1,0:T(8,128)}, u32[]{:S(2)}) copy-start(f32[512,768]{1,0:T(8,128)} %maximum_convert_fusion) | copy-start | bytes 4718596
  91.7 15.3 %copy-start.23 = (bf16[768,768]{1,0:T(8,128)(2,1)S(1)}, bf16[768,768]{1,0:T(8,128)(2,1)}, u32[]{:S(2)}) copy-start(bf16[768,768]{1,0:T(8,128)(2,1)} %param.18) | copy-start | bytes 3538948
  110.1 23.6 %copy-start.2 = (f32[640,768]{1,0:T(8,128)}, f32[640,768]{1,0:T(8,128)S(1)}, u32[]{:S(2)}) copy-start(f32[640,768]{1,0:T(8,128)S(1)} %get-tuple-element.65) | copy-start | bytes 5898244
  110.4 31.6 %copy-start.24 = (bf16[640,768]{1,0:T(8,128)(2,1)}, bf16[640,768]{1,0:T(8,128)(2,1)S(1)}, u32[]{:S(2)}) copy-start(bf16[640,768]{1,0:T(8,128)(2,1)S(1)} %multiply_convert_fusion.2) | copy-start | bytes 2949124
  129.5 4.2 copy-start.6
  146.0 42.4 %collective-permute-start.11 = (bf16[512,384]{1,0:T(8,128)(2,1)}, bf16[512,384]{1,0:T(8,128)(2,1)S(1)}, u32[]{:S(2)}, u32[]{:S(2)}) collective-permute-start(bf16[512,384]{1,0:T(8,128)(2,1)} %convolution_convert_fusion.4), channel_id=1, source_target_pairs={{0,1},{1,0},{2,3},{3,2},{4,5},{5,4},{6,7},{7,6},{8,9},{9,8},{10,11... | collective-permute-start | bytes 1179656 | tf_op jit(solution)/shard_map/ppermute | solution.py:352
  146.5 9.0 %copy-start.34 = (bf16[768,768]{1,0:T(8,128)(2,1)S(1)}, bf16[768,768]{1,0:T(8,128)(2,1)}, u32[]{:S(2)}) copy-start(bf16[768,768]{1,0:T(8,128)(2,1)} %wk_ref.3) | copy-start | bytes 3538948
  161.1 329.0 %all-reduce.4.cloned.1.call-start = ((), (), s32[]{:S(2)}) async-start(), calls=%async_computation.3 | async-start | bytes 28311552 | tf_op jit(solution)/shard_map/psum | solution.py:331
  161.2 8.4 %copy-start.40 = (f32[640]{0:T(1024)S(1)}, f32[640]{0:T(1024)}, u32[]{:S(2)}) copy-start(f32[640]{0:T(1024)} %get-tuple-element.70) | copy-start | bytes 7684
  161.2 8.3 %copy-start.41 = (f32[640]{0:T(1024)S(1)}, f32[640]{0:T(1024)}, u32[]{:S(2)}) copy-start(f32[640]{0:T(1024)} %get-tuple-element.71) | copy-start | bytes 7684
  161.2 8.3 %copy-start.42 = (f32[640]{0:T(1024)S(1)}, f32[640]{0:T(1024)}, u32[]{:S(2)}) copy-start(f32[640]{0:T(1024)} %get-tuple-element.44) | copy-start | bytes 7684
  161.2 8.3 %copy-start.43 = (f32[640]{0:T(1024)S(1)}, f32[640]{0:T(1024)}, u32[]{:S(2)}) copy-start(f32[640]{0:T(1024)} %get-tuple-element.45) | copy-start | bytes 7684
  161.2 8.3 %copy-start.47 = (pred[512]{0:T(512)(128)(4,1)S(1)}, pred[512]{0:T(512)(128)(4,1)}, u32[]{:S(2)}) copy-start(pred[512]{0:T(512)(128)(4,1)} %compare_bitcast_fusion) | copy-start | bytes 1540
  161.2 8.3 %copy-start.48 = (pred[128]{0:T(512)(128)(4,1)S(1)}, pred[128]{0:T(512)(128)(4,1)}, u32[]{:S(2)}) copy-start(pred[128]{0:T(512)(128)(4,1)} %add_compare_fusion.1) | copy-start | bytes 388
  161.2 9.6 %copy-start.51 = (bf16[1024,768]{1,0:T(8,128)(2,1)S(1)}, bf16[1024,768]{1,0:T(8,128)(2,1)}, u32[]{:S(2)}) copy-start(bf16[1024,768]{1,0:T(8,128)(2,1)} %all-gather.2.cloned.1.call-done.fik_ref) | copy-start | bytes 4718596
  161.2 9.6 %copy-start.54 = (bf16[1024,768]{1,0:T(8,128)(2,1)S(1)}, bf16[1024,768]{1,0:T(8,128)(2,1)}, u32[]{:S(2)}) copy-start(bf16[1024,768]{1,0:T(8,128)(2,1)} %get-tuple-element.39) | copy-start | bytes 4718596
  163.2 54.7 %collective-permute-start.5 = (bf16[128,768]{1,0:T(8,128)(2,1)}, bf16[128,768]{1,0:T(8,128)(2,1)S(1)}, u32[]{:S(2)}, u32[]{:S(2)}) collective-permute-start(bf16[128,768]{1,0:T(8,128)(2,1)} %get-tuple-element.82), channel_id=1, source_target_pairs={{0,6},{1,7},{2,0},{3,1},{4,2},{5,3},{6,4},{7,5},{8,14},{9,15},{10,... | collective-permute-start | bytes 589832 | tf_op jit(solution)/shard_map/ppermute | solution.py:245
  168.9 49.6 %collective-permute-start.6 = (bf16[128,768]{1,0:T(8,128)(2,1)}, bf16[128,768]{1,0:T(8,128)(2,1)S(1)}, u32[]{:S(2)}, u32[]{:S(2)}) collective-permute-start(bf16[128,768]{1,0:T(8,128)(2,1)} %get-tuple-element.81), channel_id=1, source_target_pairs={{0,4},{1,5},{2,6},{3,7},{4,0},{5,1},{6,2},{7,3},{8,12},{9,13},{10,... | collective-permute-start | bytes 589832 | tf_op jit(solution)/shard_map/ppermute | solution.py:245
  168.9 50.3 %collective-permute-start.7 = (bf16[128,768]{1,0:T(8,128)(2,1)}, bf16[128,768]{1,0:T(8,128)(2,1)S(1)}, u32[]{:S(2)}, u32[]{:S(2)}) collective-permute-start(bf16[128,768]{1,0:T(8,128)(2,1)} %get-tuple-element.79), channel_id=1, source_target_pairs={{0,2},{1,3},{2,4},{3,5},{4,6},{5,7},{6,0},{7,1},{8,10},{9,11},{10,... | collective-permute-start | bytes 589832 | tf_op jit(solution)/shard_map/ppermute | solution.py:245
  173.0 4.0 copy-start.59
  177.0 8.5 %copy-start.52 = (bf16[1024,768]{1,0:T(8,128)(2,1)S(1)}, bf16[1024,768]{1,0:T(8,128)(2,1)}, u32[]{:S(2)}) copy-start(bf16[1024,768]{1,0:T(8,128)(2,1)} %get-tuple-element.38) | copy-start | bytes 4718596
  189.3 19.2 %copy-start.10 = (bf16[512,768]{1,0:T(8,128)(2,1)S(1)}, bf16[512,768]{1,0:T(8,128)(2,1)}, u32[]{:S(2)}) copy-start(bf16[512,768]{1,0:T(8,128)(2,1)} %copy-done.9) | copy-start | bytes 2359300
  189.3 19.2 %copy-start.27 = (bf16[512,768]{1,0:T(8,128)(2,1)S(1)}, bf16[512,768]{1,0:T(8,128)(2,1)}, u32[]{:S(2)}) copy-start(bf16[512,768]{1,0:T(8,128)(2,1)} %copy-done.26) | copy-start | bytes 2359300
  208.5 3.5 copy-start.28
  224.6 2.4 collective-permute-start.12
  236.0 54.9 %collective-permute-start.13 = (bf16[128,768]{1,0:T(8,128)(2,1)S(1)}, bf16[128,768]{1,0:T(8,128)(2,1)S(1)}, u32[]{:S(2)}, u32[]{:S(2)}) collective-permute-start(bf16[128,768]{1,0:T(8,128)(2,1)S(1)} %get-tuple-element.75), channel_id=1, source_target_pairs={{0,6},{1,7},{2,0},{3,1},{4,2},{5,3},{6,4},{7,5},{8,14},{9,15},{10,... | collective-permute-start | bytes 589832 | tf_op jit(solution)/shard_map/ppermute | solution.py:245
  239.5 51.5 %collective-permute-start.14 = (bf16[128,768]{1,0:T(8,128)(2,1)S(1)}, bf16[128,768]{1,0:T(8,128)(2,1)S(1)}, u32[]{:S(2)}, u32[]{:S(2)}) collective-permute-start(bf16[128,768]{1,0:T(8,128)(2,1)S(1)} %get-tuple-element.74), channel_id=1, source_target_pairs={{0,4},{1,5},{2,6},{3,7},{4,0},{5,1},{6,2},{7,3},{8,12},{9,13},{10,... | collective-permute-start | bytes 589832 | tf_op jit(solution)/shard_map/ppermute | solution.py:245
  240.4 50.5 %collective-permute-start.15 = (bf16[128,768]{1,0:T(8,128)(2,1)S(1)}, bf16[128,768]{1,0:T(8,128)(2,1)S(1)}, u32[]{:S(2)}, u32[]{:S(2)}) collective-permute-start(bf16[128,768]{1,0:T(8,128)(2,1)S(1)} %get-tuple-element.72), channel_id=1, source_target_pairs={{0,2},{1,3},{2,4},{3,5},{4,6},{5,7},{6,0},{7,1},{8,10},{9,11},{10,... | collective-permute-start | bytes 589832 | tf_op jit(solution)/shard_map/ppermute | solution.py:245
  490.1 5.6 %copy-start.12 = (bf16[768,2048]{1,0:T(8,128)(2,1)S(1)}, bf16[768,2048]{1,0:T(8,128)(2,1)}, u32[]{:S(2)}) copy-start(bf16[768,2048]{1,0:T(8,128)(2,1)} %get-tuple-element.62) | copy-start | bytes 9437188
  495.7 3.6 copy-start.11
  505.7 3.8 copy-start.1
  (31 other events, 63.5 us)
Sparse Core Ops, SparseCore 0:
  19.6 37.7 all-gather.1
  161.2 43.3 reduce-scatter.1
  218.0 272.0 all-reduce.3

commit v2 on v1

v2 whole, which is shorter than its diff:
```python
import functools
import math

import jax
import jax.numpy as jnp
from jax import lax
from jax.experimental import pallas as pl
from jax.experimental.pallas import tpu as pltpu
from jax.sharding import PartitionSpec as P

HEADS = 12
GROUPS = 4
SHARDS = 16
EPS = 1e-06
NEG = -1000000000.0
LOG2E = 1.4426950408889634
LN2 = 0.6931471805599453
GELU_C = 0.7978845608028654
GELU_A = 0.044715
BF = jnp.bfloat16
F32 = jnp.float32
VMEM_LIMIT = 56 * 1024 * 1024
ANY = pl.BlockSpec(memory_space=pl.ANY)


def dot(left, right):
    return jnp.dot(left, right, preferred_element_type=F32)


def dot_nt(left, right):
    return lax.dot_general(left, right, (((1,), (1,)), ((), ())), preferred_element_type=F32)


def dot_tn(left, right):
    return lax.dot_general(left, right, (((0,), (0,)), ((), ())), preferred_element_type=F32)


def split_three(column):
    hi = column.astype(BF).astype(F32)
    rest = column - hi
    mid = rest.astype(BF).astype(F32)
    return hi, mid, rest - mid


def extras(rows, columns):
    lane = lax.broadcasted_iota(jnp.int32, (rows, 128), 1)
    out = jnp.zeros((rows, 128), F32)
    for index, column in enumerate(columns):
        if column is not None:
            out = jnp.where(lane == index, column, out)
    return out.astype(BF)


def head_lanes(values, half):
    lane = lax.broadcasted_iota(jnp.int32, values.shape, 1)
    return jnp.where((lane < 64) if half == 0 else (lane >= 64), values, jnp.zeros_like(values))


def stack_heads(values):
    return jnp.concatenate([head_lanes(values, 0), head_lanes(values, 1)], axis=0)


def attend_kernel(q_rows, place_ref, fiq_ref, fik_ref, wq_ref, wk_ref, wv_ref, ext_ref, *refs):
    q_ref, k_ref, v_ref, log_ref, out_ref = refs[-5:]
    scale = LOG2E / math.sqrt(64.0)
    both = dot(fik_ref[...], jnp.concatenate([wk_ref[...], wv_ref[...]], axis=1)).astype(BF)
    k_ref[0] = both[:, :128]
    v_ref[0] = both[:, 128:]
    query = (dot(fiq_ref[...], wq_ref[...]) * scale).astype(BF)
    q_ref[0] = query
    ext = ext_ref[...]
    keys = jnp.concatenate([both[:, :128], ext], axis=1)
    values = jnp.concatenate([both[:, 128:], ext], axis=1)
    one = extras(2 * q_rows, (None, None, None, 1.0))
    for start in range(0, fiq_ref.shape[0], q_rows):
        rows = slice(start, start + q_rows)
        scores = dot_nt(jnp.concatenate([stack_heads(query[rows]), one], axis=1), keys)
        top = jnp.max(scores, axis=1, keepdims=True)
        weights = jnp.exp2(scores - top).astype(BF)
        mixed = dot(weights, values)
        norm = mixed[:, 128:129]
        logs = extras(2 * q_rows, split_three(-(top + jnp.log2(norm))) + (1.0,))
        log_ref[0, rows, :] = logs[:q_rows]
        log_ref[1, rows, :] = logs[q_rows:]
        scaled = mixed[:, :128] / norm
        lane = lax.broadcasted_iota(jnp.int32, (q_rows, 128), 1)
        out_ref[rows, :] = jnp.where(lane < 64, scaled[:q_rows], scaled[q_rows:]).astype(BF)


def attend(place, fi_q, fi_k, w_query, w_key, w_value, ext, pairs, q_rows, after=()):
    q_total, width = fi_q.shape
    k_total = fi_k.shape[0]
    column = lambda i, p: (0, p[0] * pairs + i)
    whole = lambda i, p: (0, 0)
    stacked = lambda i, p: (i, 0, 0)
    return pl.pallas_call(
        functools.partial(attend_kernel, q_rows),
        grid_spec=pltpu.PrefetchScalarGridSpec(
            num_scalar_prefetch=1,
            grid=(pairs,),
            in_specs=[
                pl.BlockSpec((q_total, width), whole),
                pl.BlockSpec((k_total, width), whole),
                pl.BlockSpec((width, 128), column),
                pl.BlockSpec((width, 128), column),
                pl.BlockSpec((width, 128), column),
                pl.BlockSpec((k_total, 128), whole),
            ] + [ANY] * len(after),
            out_specs=[
                pl.BlockSpec((1, q_total, 128), stacked),
                pl.BlockSpec((1, k_total, 128), stacked),
                pl.BlockSpec((1, k_total, 128), stacked),
                pl.BlockSpec((2, q_total, 128), stacked),
                pl.BlockSpec((q_total, 128), lambda i, p: (0, i)),
            ],
        ),
        out_shape=[
            jax.ShapeDtypeStruct((pairs, q_total, 128), BF),
            jax.ShapeDtypeStruct((pairs, k_total, 128), BF),
            jax.ShapeDtypeStruct((pairs, k_total, 128), BF),
            jax.ShapeDtypeStruct((2 * pairs, q_total, 128), BF),
            jax.ShapeDtypeStruct((q_total, pairs * 128), BF),
        ],
        compiler_params=pltpu.CompilerParams(vmem_limit_bytes=VMEM_LIMIT),
        cost_estimate=pl.CostEstimate(
            flops=4 * 128 * pairs * (4 * q_total * k_total + width * (q_total + 2 * k_total)),
            bytes_accessed=2 * (q_total + k_total) * width * 4,
            transcendentals=2 * pairs * q_total * k_total,
        ),
    )(place, fi_q, fi_k, w_query, w_key, w_value, ext, *after)


def attend_back_kernel(q_rows, q_ref, k_ref, v_ref, ext_ref, log_ref, out_ref, grad_ref, *refs):
    dq_ref, dk_ref, dv_ref = refs[-3:]
    ext = ext_ref[...]
    key_pair = k_ref[0]
    keys = jnp.concatenate([key_pair, ext], axis=1)
    values = jnp.concatenate([v_ref[0], ext], axis=1)
    keys_trans = jnp.transpose(key_pair.astype(F32)).astype(BF)
    dk_sum = jnp.zeros(key_pair.shape, F32)
    dv_sum = jnp.zeros(key_pair.shape, F32)
    for start in range(0, q_ref.shape[1], q_rows):
        rows = slice(start, start + q_rows)
        grad = grad_ref[rows, :]
        product = grad.astype(F32) * out_ref[rows, :].astype(F32)
        delta = jnp.sum(stack_heads(product), axis=1, keepdims=True)
        grad_h = stack_heads(grad)
        query_h = stack_heads(q_ref[0, rows, :])
        logs = jnp.concatenate([log_ref[0, rows, :], log_ref[1, rows, :]], axis=0)
        probs = jnp.exp2(dot_nt(keys, jnp.concatenate([query_h, logs], axis=1)))
        centred = dot_nt(values, jnp.concatenate([grad_h, extras(2 * q_rows, split_three(-delta))], axis=1))
        grad_scores = (probs * centred).astype(BF)
        dv_sum = dv_sum + dot(probs.astype(BF), grad_h)
        dk_sum = dk_sum + dot(grad_scores, query_h)
        first = dot(keys_trans[:64], grad_scores[:, :q_rows])
        second = dot(keys_trans[64:], grad_scores[:, q_rows:])
        dq_ref[rows, :] = (jnp.transpose(jnp.concatenate([first, second], axis=0)) * 0.125).astype(BF)
    dk_ref[...] = (dk_sum * LN2).astype(BF)
    dv_ref[...] = dv_sum.astype(BF)


def attend_back(query, key, value, ext, logs, out, grad, q_rows, after=()):
    _, q_total, _ = query.shape
    pairs = query.shape[0]
    k_total = key.shape[1]
    stacked = lambda i: (i, 0, 0)
    flat = lambda i: (0, i)
    return pl.pallas_call(
        functools.partial(attend_back_kernel, q_rows),
        grid=(pairs,),
        in_specs=[
            pl.BlockSpec((1, q_total, 128), stacked),
            pl.BlockSpec((1, k_total, 128), stacked),
            pl.BlockSpec((1, k_total, 128), stacked),
            pl.BlockSpec((k_total, 128), lambda i: (0, 0)),
            pl.BlockSpec((2, q_total, 128), stacked),
            pl.BlockSpec((q_total, 128), flat),
            pl.BlockSpec((q_total, 128), flat),
        ] + [ANY] * len(after),
        out_specs=[
            pl.BlockSpec((q_total, 128), lambda i: (0, i)),
            pl.BlockSpec((k_total, 128), lambda i: (0, i)),
            pl.BlockSpec((k_total, 128), lambda i: (0, i)),
        ],
        out_shape=[
            jax.ShapeDtypeStruct((q_total, pairs * 128), BF),
            jax.ShapeDtypeStruct((k_total, pairs * 128), BF),
            jax.ShapeDtypeStruct((k_total, pairs * 128), BF),
        ],
        compiler_params=pltpu.CompilerParams(vmem_limit_bytes=VMEM_LIMIT),
        cost_estimate=pl.CostEstimate(
            flops=2 * 256 * pairs * 5 * q_total * k_total,
            bytes_accessed=2 * 128 * pairs * (4 * q_total + 4 * k_total),
            transcendentals=2 * pairs * q_total * k_total,
        ),
    )(query, key, value, ext, logs, out, grad, *after)


FF_TILE = 256


def ff_kernel(first, place_ref, second_ref, grad_ref, wg_ref, wu_ref, wd_ref, *refs):
    two_ref, gs_ref, part_ref, second_t_ref = refs[-4:]
    step = pl.program_id(0)

    @pl.when(step == 0)
    def _():
        second_t_ref[...] = jnp.transpose(second_ref[...])
        if first:
            two_ref[...] = jnp.zeros_like(two_ref)
            gs_ref[...] = jnp.zeros_like(gs_ref)
        else:
            two_ref[...] = refs[0][...]
            gs_ref[...] = refs[1][...]

    second, grad = second_ref[...], grad_ref[...]
    gate = dot(second, wg_ref[...])
    up = dot(second, wu_ref[...])
    grad_inner = dot_nt(grad, wd_ref[...])
    square = gate * gate
    bend = jnp.tanh(GELU_C * gate * (1.0 + GELU_A * square))
    half_plus = 0.5 + 0.5 * bend
    gelu = gate * half_plus
    slope = half_plus + 0.5 * gate * (1.0 - bend * bend) * (GELU_C * (1.0 + 3.0 * GELU_A * square))
    inner = (gelu * up).astype(BF)
    grad_gate = (grad_inner * up * slope).astype(BF)
    grad_up = (grad_inner * gelu).astype(BF)
    two_ref[...] += dot(inner, wd_ref[...])
    gs_ref[...] += dot_nt(grad_gate, wg_ref[...]) + dot_nt(grad_up, wu_ref[...])
    width = second.shape[1]
    shard, shard_down = width // SHARDS, 2 * FF_TILE // SHARDS
    shape = (4, 4, shard, FF_TILE)
    part_gate = dot(second_t_ref[...], grad_gate).astype(BF).reshape(shape)
    part_up = dot(second_t_ref[...], grad_up).astype(BF).reshape(shape)
    part_down = dot_tn(inner, grad).astype(BF)
    for odd in range(2):
        @pl.when(step % 2 == odd)
        def _():
            part_ref[:, :, shard * odd:shard * (odd + 1), :] = part_gate
            part_ref[:, :, shard * (2 + odd):shard * (3 + odd), :] = part_up
            for tile in range(width // FF_TILE):
                at = 4 * shard + shard_down * tile
                part_ref[2 * odd:2 * odd + 2, :, at:at + shard_down, :] = (
                    part_down[:, FF_TILE * tile:FF_TILE * (tile + 1)].reshape(2, 4, shard_down, FF_TILE))


def ff_half(place, second, grad, w_gate, w_up, w_down, sums, after=()):
    rows, width = second.shape
    tiles = w_gate.shape[1] // FF_TILE // 2
    tile_at = lambda j, p: (j // 2) * 4 + p[0] * 2 + j % 2
    whole = lambda j, p: (0, 0)
    sum_spec = pl.BlockSpec((rows, width), whole)
    columns = pl.BlockSpec((width, FF_TILE), lambda j, p: (0, tile_at(j, p)))
    shard_rows = 4 * (width // SHARDS) + (2 * FF_TILE // SHARDS) * (width // FF_TILE)
    return pl.pallas_call(
        functools.partial(ff_kernel, sums is None),
        grid_spec=pltpu.PrefetchScalarGridSpec(
            num_scalar_prefetch=1,
            grid=(tiles,),
            in_specs=[
                pl.BlockSpec((rows, width), whole), pl.BlockSpec((rows, width), whole),
                columns, columns, pl.BlockSpec((FF_TILE, width), lambda j, p: (tile_at(j, p), 0)),
            ] + [sum_spec] * (0 if sums is None else 2) + [ANY] * len(after),
            out_specs=[sum_spec, sum_spec,
                       pl.BlockSpec((4, 4, shard_rows, FF_TILE), lambda j, p: (0, 0, j // 2, 0))],
            scratch_shapes=[pltpu.VMEM((width, rows), BF)],
        ),
        out_shape=[jax.ShapeDtypeStruct((rows, width), F32)] * 2
        + [jax.ShapeDtypeStruct((4, 4, 2 * shard_rows, FF_TILE), BF)],
        compiler_params=pltpu.CompilerParams(vmem_limit_bytes=VMEM_LIMIT),
        cost_estimate=pl.CostEstimate(
            flops=18 * rows * width * tiles * FF_TILE,
            bytes_accessed=12 * width * tiles * FF_TILE + 16 * rows * width,
            transcendentals=rows * tiles * FF_TILE),
    )(place, second, grad, w_gate, w_up, w_down, *(sums or ()), *after)


def split_kernel(place_ref, *refs):
    ins, outs = refs[:8], refs[-4:]
    for index, out in enumerate(outs):
        for step in range(4):
            at = jnp.bitwise_xor(place_ref[3], step)
            out[0, step] = (ins[index][0, 0, at].astype(F32) + ins[4 + index][0, 0, at].astype(F32)).astype(BF)


def split_cores(place, kept, got, after=()):
    tail = kept.shape[3:]

    def spec(order, away):
        def at(b, p):
            first, second = p[1 + order] ^ away, p[2 - order] ^ b
            return (order, first + 2 * second if order == 0 else second + 2 * first, 0, 0, 0)
        return pl.BlockSpec((1, 1, 4) + tail, at)

    specs = [spec(order, away) for order in range(2) for away in range(2)]
    out = pl.BlockSpec((1, 4) + tail, lambda b, p: (b, 0, 0, 0))
    return pl.pallas_call(
        split_kernel,
        grid_spec=pltpu.PrefetchScalarGridSpec(
            num_scalar_prefetch=1, grid=(2,), in_specs=specs * 2 + [ANY] * len(after), out_specs=[out] * 4),
        out_shape=[jax.ShapeDtypeStruct((2, 4) + tail, BF)] * 4,
        compiler_params=pltpu.CompilerParams(vmem_limit_bytes=VMEM_LIMIT),
        cost_estimate=pl.CostEstimate(flops=0, bytes_accessed=6 * kept.size, transcendentals=0),
    )(place, *([kept] * 4), *([got] * 4), *after)


def hold(array, after):
    return pl.pallas_call(
        lambda *refs: None,
        in_specs=[ANY] * (1 + len(after)),
        out_specs=ANY,
        out_shape=jax.ShapeDtypeStruct(array.shape, array.dtype),
        input_output_aliases={0: 0},
        cost_estimate=pl.CostEstimate(flops=0, bytes_accessed=0, transcendentals=0),
    )(array, *after)


def place_rows_kernel(place_ref, *refs):
    pieces, out_ref = refs[:-1], refs[-1]
    for step in range(GROUPS):
        out_ref[(place_ref[3] + step) % GROUPS] = pieces[step][...]
    for index in range(GROUPS, len(pieces)):
        out_ref[index] = pieces[index][...]


def place_rows(place, pieces):
    block = pl.BlockSpec(pieces[0].shape, lambda j, p: (0, 0))
    shape = (len(pieces),) + pieces[0].shape
    return pl.pallas_call(
        place_rows_kernel,
        grid_spec=pltpu.PrefetchScalarGridSpec(
            num_scalar_prefetch=1, grid=(1,), in_specs=[block] * len(pieces),
            out_specs=pl.BlockSpec(shape, lambda j, p: (0, 0, 0))),
        out_shape=jax.ShapeDtypeStruct(shape, pieces[0].dtype),
        cost_estimate=pl.CostEstimate(flops=0, bytes_accessed=0, transcendentals=0),
    )(place, *pieces)


def add_kernel(x_ref, rx_ref, y_ref, ry_ref, *refs):
    outs = refs[-4:]
    for index in range(2):
        outs[index][...] = add_low(x_ref[index], rx_ref[index])
        outs[2 + index][...] = add_low(y_ref[index], ry_ref[index])


def add_pairs(x, rx, y, ry, after=()):
    tail = x.shape[2:]
    return pl.pallas_call(
        add_kernel,
        grid=(4,),
        in_specs=[pl.BlockSpec((2, 1) + tail, lambda j: (0, j, 0, 0))] * 4 + [ANY] * len(after),
        out_specs=[pl.BlockSpec((1,) + tail, lambda j: (j, 0, 0))] * 4,
        out_shape=[jax.ShapeDtypeStruct((4,) + tail, BF)] * 4,
        compiler_params=pltpu.CompilerParams(vmem_limit_bytes=VMEM_LIMIT),
        cost_estimate=pl.CostEstimate(flops=0, bytes_accessed=12 * x.size, transcendentals=0),
    )(x, rx, y, ry, *after)


def add_four_kernel(x_ref, rx_ref, y_ref, ry_ref, *refs):
    outs = refs[-4:]
    for index in range(4):
        outs[index][0] = add_low(x_ref[index], rx_ref[index])
        outs[index][1] = add_low(y_ref[index], ry_ref[index])


def add_fours(x, rx, y, ry, after=()):
    tail = x.shape[1:]
    whole = pl.BlockSpec(x.shape, lambda j: (0, 0, 0))
    return pl.pallas_call(
        add_four_kernel,
        grid=(1,),
        in_specs=[whole] * 4 + [ANY] * len(after),
        out_specs=[pl.BlockSpec((2,) + tail, lambda j: (0, 0, 0))] * 4,
        out_shape=[jax.ShapeDtypeStruct((2,) + tail, BF)] * 4,
        compiler_params=pltpu.CompilerParams(vmem_limit_bytes=VMEM_LIMIT),
        cost_estimate=pl.CostEstimate(flops=0, bytes_accessed=12 * x.size, transcendentals=0),
    )(x, rx, y, ry, *after)


def sum_kernel(*refs):
    total = refs[0][...].astype(F32)
    for ref in refs[1:GROUPS]:
        total = total + ref[...].astype(F32)
    refs[-1][...] = total.astype(BF)


def sum_shards(shards, after=()):
    whole = pl.BlockSpec(shards[0].shape, lambda: (0, 0, 0))
    return pl.pallas_call(
        sum_kernel,
        in_specs=[whole] * GROUPS + [ANY] * len(after),
        out_specs=whole,
        out_shape=jax.ShapeDtypeStruct(shards[0].shape, BF),
        cost_estimate=pl.CostEstimate(flops=0, bytes_accessed=0, transcendentals=0),
    )(*shards, *after)


def stack_orders_kernel(*refs):
    for order in range(2):
        for index in range(GROUPS):
            refs[order - 2][index] = refs[index][order]


def stack_orders(pieces, after=()):
    tail = pieces[0].shape[1:]
    return pl.pallas_call(
        stack_orders_kernel,
        in_specs=[pl.BlockSpec((2,) + tail, lambda: (0, 0, 0))] * GROUPS + [ANY] * len(after),
        out_specs=[pl.BlockSpec((GROUPS,) + tail, lambda: (0, 0, 0))] * 2,
        out_shape=[jax.ShapeDtypeStruct((GROUPS,) + tail, BF)] * 2,
        cost_estimate=pl.CostEstimate(flops=0, bytes_accessed=0, transcendentals=0),
    )(*pieces, *after)


def stack_pairs_kernel(x_ref, rx_ref, y_ref, ry_ref, *refs):
    refs[-2][0] = x_ref[...]
    refs[-2][1] = rx_ref[...]
    refs[-1][0] = y_ref[...]
    refs[-1][1] = ry_ref[...]


def stack_pairs(x, rx, y, ry, after=()):
    tail = x.shape[1:]
    block = pl.BlockSpec((1,) + tail, lambda j: (j, 0, 0))
    return pl.pallas_call(
        stack_pairs_kernel,
        grid=(GROUPS,),
        in_specs=[block] * 4 + [ANY] * len(after),
        out_specs=[pl.BlockSpec((2, 1) + tail, lambda j: (0, j, 0, 0))] * 2,
        out_shape=[jax.ShapeDtypeStruct((2,) + x.shape, BF)] * 2,
        cost_estimate=pl.CostEstimate(flops=0, bytes_accessed=0, transcendentals=0),
    )(x, rx, y, ry, *after)


def grad_kernel(columns, place_ref, *refs):
    ins, part_ref = refs[:-1], refs[-1]
    for order, at, terms in columns:
        total = None
        for left, right in terms:
            term = dot_tn(ins[left][...], ins[right][...])
            total = term if total is None else total + term
        rows, cols = total.shape
        part_ref[order, :, :, :, at:at + cols] = total.astype(BF).reshape(4, 4, rows // SHARDS, cols)


def grad_part(place, ins, columns, after=()):
    specs = []
    for array, halved in ins:
        depth, cols = array.shape
        if halved:
            specs.append(pl.BlockSpec((depth, cols // 2), lambda j, p: (0, p[0])))
        else:
            specs.append(pl.BlockSpec((depth, cols), lambda j, p: (0, 0)))
    rows = ins[0][0].shape[1]
    shape = (2, 4, 4, rows // SHARDS, rows)
    return pl.pallas_call(
        functools.partial(grad_kernel, columns),
        grid_spec=pltpu.PrefetchScalarGridSpec(
            num_scalar_prefetch=1,
            grid=(1,),
            in_specs=specs + [ANY] * len(after),
            out_specs=pl.BlockSpec(shape, lambda j, p: (0, 0, 0, 0, 0)),
        ),
        out_shape=jax.ShapeDtypeStruct(shape, BF),
        compiler_params=pltpu.CompilerParams(vmem_limit_bytes=VMEM_LIMIT),
        cost_estimate=pl.CostEstimate(
            flops=sum(2 * rows * (rows // 2) * ins[left][0].shape[0]
                      for _, _, terms in columns for left, _ in terms),
            bytes_accessed=sum(2 * a.size for a, _ in ins), transcendentals=0),
    )(place, *[a for a, _ in ins], *after)


def from_pieces(place_ref, refs, order, group):
    here_ref, away_ref, other_here_ref, other_away_ref = refs[4 * order:4 * order + 4]
    quarter = pl.program_id(0)
    bit = quarter % 2 if order == 0 else quarter // 2
    near = place_ref[1 + order] == bit
    at = jnp.bitwise_xor(place_ref[3], group)
    own = jnp.where(near, here_ref[0, at], away_ref[0, at]).astype(F32)
    other = jnp.where(near, other_here_ref[0, at], other_away_ref[0, at]).astype(F32)
    lower = place_ref[0] == 0
    return jnp.where(lower, own, other), jnp.where(lower, other, own)


def assemble_ff_kernel(place_ref, own_ref, other_ref, gate_ref, up_ref, down_ref):
    shard, down = gate_ref.shape[0] // 4, down_ref.shape[2] // 4
    shard_rows = own_ref.shape[2] // 2

    def write(halves):
        for group in range(4):
            rows = slice(shard * group, shard * (group + 1))
            for half, source in enumerate(halves):
                for order in range(2):
                    base = order * shard_rows
                    for tile in range(2):
                        at = ((order * 2 + half) * 2 + tile) * FF_TILE
                        gate_ref[rows, at:at + FF_TILE] = source[
                            0, group, base + shard * tile:base + shard * (tile + 1)].astype(F32)
                        up_ref[rows, at:at + FF_TILE] = source[
                            0, group, base + shard * (2 + tile):base + shard * (3 + tile)].astype(F32)
                    for tile in range(down_ref.shape[3] // FF_TILE):
                        at = base + 4 * shard + down * tile
                        down_ref[order * 2 + half, 0, down * group:down * (group + 1),
                                 FF_TILE * tile:FF_TILE * (tile + 1)] = source[
                                     0, group, at:at + down].astype(F32)

    pl.when(place_ref[0] == 0)(lambda: write((own_ref, other_ref)))
    pl.when(place_ref[0] != 0)(lambda: write((other_ref, own_ref)))


def assemble_ff(place, own, other, hidden):
    quarter = lambda rows: pl.BlockSpec((rows, hidden), lambda q, p: (q, 0))
    part = pl.BlockSpec((1,) + own.shape[1:], lambda q, p: (q, 0, 0, 0))
    rows = own.shape[2] // 2
    width = (rows * FF_TILE * SHARDS * 4) // (3 * hidden)
    gate, up, down = pl.pallas_call(
        assemble_ff_kernel,
        grid_spec=pltpu.PrefetchScalarGridSpec(
            num_scalar_prefetch=1, grid=(4,), in_specs=[part, part],
            out_specs=[quarter(width // 4), quarter(width // 4),
                       pl.BlockSpec((4, 1, hidden // 16, width), lambda q, p: (0, q, 0, 0))]),
        out_shape=[jax.ShapeDtypeStruct((width, hidden), F32)] * 2
        + [jax.ShapeDtypeStruct((4, 4, hidden // 16, width), F32)],
        compiler_params=pltpu.CompilerParams(vmem_limit_bytes=VMEM_LIMIT),
        cost_estimate=pl.CostEstimate(flops=0, bytes_accessed=12 * own.size, transcendentals=0),
    )(place, own, other)
    return gate, up, down.reshape(hidden, width)


def assemble_kernel(place_ref, *refs):
    outs = refs[-4:]
    shard = outs[0].shape[0] // 4
    for order in range(2):
        for group in range(4):
            rows = slice(shard * group, shard * (group + 1))
            for half, value in enumerate(from_pieces(place_ref, refs, order, group)):
                width = value.shape[1] // 2
                for which in range(2):
                    outs[2 * order + which][rows, half * width:(half + 1) * width] = (
                        value[:, which * width:(which + 1) * width])


def assemble(kernel, place, pieces, out_shapes, out_specs, after=()):
    tail = pieces[0].shape[1:]
    near = pl.BlockSpec((1,) + tail, lambda q, p: (p[2] ^ (q // 2), 0, 0, 0))
    far = pl.BlockSpec((1,) + tail, lambda q, p: (p[1] ^ (q % 2), 0, 0, 0))
    return pl.pallas_call(
        kernel,
        grid_spec=pltpu.PrefetchScalarGridSpec(
            num_scalar_prefetch=1, grid=(4,), in_specs=[near] * 4 + [far] * 4 + [ANY] * len(after),
            out_specs=out_specs),
        out_shape=[jax.ShapeDtypeStruct(shape, F32) for shape in out_shapes],
        compiler_params=pltpu.CompilerParams(vmem_limit_bytes=VMEM_LIMIT),
        cost_estimate=pl.CostEstimate(
            flops=0, bytes_accessed=16 * 8 * pieces[0].size // 4, transcendentals=0),
    )(place, *pieces, *after)


def add_low(left, right):
    return (left.astype(F32) + right.astype(F32)).astype(BF)


def norm_scale(values):
    return lax.rsqrt(jnp.mean(values * values, axis=-1, keepdims=True) + EPS)


def norm_back(values, gain, grad):
    scale = norm_scale(values)
    scaled = values * scale
    weighted = grad * gain
    inner = jnp.mean(weighted * scaled, axis=-1, keepdims=True)
    return scale * (weighted - scaled * inner), jnp.sum(grad * scaled, axis=0)


def masked_squares(values_in, row_mask):
    return jnp.sum(row_mask * jnp.sum(values_in * values_in, axis=-1))


def body(n_img, n_seq, patches, counts, norm_gain_one, w_query, w_key, w_value, w_out,
         norm_gain_two, w_gate, w_up, w_down, cotangent):
    charts, block_len, width = patches.shape
    members = n_seq // GROUPS
    head_count = HEADS // members
    pairs = -(-head_count // 2)
    pad_cols = pairs * 128 - head_count * 64
    mine_cols = head_count * 64
    main_own = GROUPS * block_len
    seq_len = n_seq * block_len
    here = lax.axis_index("seq")
    group, member = here // members, here % members
    img_here = lax.axis_index("img")

    def slot_of(who):
        return (who % 2) * (members // 2) + who // 2

    def bit_exchange(axis, bit):
        def move(array):
            if axis == "img":
                perm = [(i, i ^ (1 << bit)) for i in range(n_img)]
            elif axis == "group":
                perm = [(g * members + r, (g ^ (1 << bit)) * members + r)
                        for g in range(GROUPS) for r in range(members)]
            else:
                perm = [(g * members + r, g * members + (r ^ (1 << bit)))
                        for g in range(GROUPS) for r in range(members)]
            return lax.ppermute(array, "img" if axis == "img" else "seq", perm)
        return move

    img_moves = [bit_exchange("img", 0), bit_exchange("img", 1)]
    z_moves = [bit_exchange("group", 0), bit_exchange("group", 1)]

    def z_move(array, step):
        perm = [(g * members + r, (g ^ step) * members + r) for g in range(GROUPS) for r in range(members)]
        return lax.ppermute(array, "seq", perm)

    core_move = bit_exchange("member", 0)
    more_moves = [bit_exchange("img", b) for b in range(2, n_img.bit_length() - 1)]
    more_moves += [bit_exchange("member", b) for b in range(1, members.bit_length() - 1)]
    img_bits = [img_here % 2, (img_here // 2) % 2]
    half_here = member % 2

    def place_of(half):
        return jnp.stack([half] + img_bits + [group]).astype(jnp.int32)

    there, here_place = place_of(1 - half_here), place_of(half_here)

    def sum_img_first(kx, sx, ky, sy, after=()):
        return add_pairs(kx, img_moves[0](sx), ky, img_moves[1](sy), after)

    def sum_img_second(kx, sx, ky, sy, after=()):
        return add_fours(kx, img_moves[1](sx), ky, img_moves[0](sy), after)

    def sum_groups(shards, after=()):
        total = sum_shards(
            [shards[0]] + [z_move(shards[step], step) for step in range(1, GROUPS)], after)
        for move in more_moves:
            total = add_low(total, move(total))
        return total

    def quarters(total, after):
        return stack_orders([total] + [z_move(total, step) for step in range(1, GROUPS)], after)

    def halves(parts, after):
        return stack_pairs(parts[0], img_moves[1](parts[0]), parts[1], img_moves[0](parts[1]), after)

    def far_halves(near, after):
        far = [img_moves[order](near[order]) for order in range(2)]
        return [hold(f, after) for f in far] if after else far

    def every_piece(near, far):
        return [a for n, f in zip(near, far) for a in (n, f, core_move(n), core_move(f))]

    def shift_perm(step):
        return [(g * members + r, ((g + step) % GROUPS) * members + r)
                for g in range(GROUPS) for r in range(members)]

    def member_perm(step):
        return [(g * members + r, g * members + (r ^ step))
                for g in range(GROUPS) for r in range(members)]

    def to_groups(array, after=()):
        pieces = []
        for step in range(GROUPS):
            part = lax.dynamic_index_in_dim(array, (group + step) % GROUPS, 0, keepdims=False)
            if step:
                part = lax.ppermute(hold(part, after) if after else part, "seq", shift_perm(step))
            pieces.append(part)
        return pieces

    def from_groups(rows):
        pieces = []
        for step in range(GROUPS):
            part = rows[step * block_len:(step + 1) * block_len]
            pieces.append(part if step == 0 else lax.ppermute(part, "seq", shift_perm(-step)))
        return place_rows(here_place, pieces + [rows[main_own:]])

    def to_members(own):
        return [own] + [lax.ppermute(own, "seq", member_perm(step)) for step in range(1, members)]

    def columns_of(weight, who):
        part = lax.dynamic_slice_in_dim(weight, who * mine_cols, mine_cols, 1)
        return jnp.pad(part, ((0, 0), (0, pad_cols))) if pad_cols else part

    gain_one = norm_gain_one.astype(F32)
    gain_two = norm_gain_two.astype(F32)
    steps = jnp.arange(GROUPS, dtype=jnp.int32)
    block_of = ((group - steps) % GROUPS) * members
    inside = jnp.arange(block_len, dtype=jnp.int32)

    def main_positions(who):
        return ((block_of + who) * block_len)[:, None] + inside[None, :]

    count_main = lax.dynamic_index_in_dim(counts, group, 0, keepdims=False)
    count_rest = counts[GROUPS]
    rest_positions = here * block_len + inside
    row_valid = jnp.concatenate([
        (main_positions(member) < count_main).reshape(-1), rest_positions < count_rest])
    row_mask = row_valid.astype(F32)
    key_positions = jnp.concatenate(
        [main_positions(member ^ step).reshape(-1) for step in range(members)])

    def key_extras(valid):
        bias = jnp.where(valid, 0.0, NEG)[:, None]
        lane = jnp.arange(128)[None, :]
        return jnp.where(lane < 3, 1.0, jnp.where(lane == 3, bias, 0.0)).astype(BF)

    ext_main = key_extras(key_positions < count_main)
    ext_rest = key_extras(jnp.arange(seq_len) < count_rest)

    rest_rows = patches[GROUPS]
    rest_f32 = rest_rows.astype(F32)
    first_rest = (rest_f32 * norm_scale(rest_f32) * gain_one).astype(BF)
    moved = to_groups(patches)
    main_rows = jnp.concatenate(moved, axis=0).astype(F32)
    first_main = (main_rows * norm_scale(main_rows) * gain_one).astype(BF)
    first_all = jnp.concatenate(to_members(first_main), axis=0)
    first_rest_sent, _ = lax.optimization_barrier((first_rest, first_main))
    first_rest_all = lax.all_gather(first_rest_sent, "seq", axis=0, tiled=True)

    place = jnp.reshape(slot_of(member), (1,)).astype(jnp.int32)
    zero_place = jnp.zeros((1,), jnp.int32)
    if pad_cols:
        main_weights = [columns_of(w, slot_of(member)) for w in (w_query, w_key, w_value)]
        main_place = zero_place
    else:
        main_weights = [w_query, w_key, w_value]
        main_place = place
    q_rows = min(128, block_len)
    query_main, key_main, value_main, logs_main, attn_main = attend(
        main_place, first_all, first_all, *main_weights, ext_main, pairs, q_rows)
    query_rest, key_rest, value_rest, logs_rest, attn_rest = attend(
        zero_place, first_rest, first_rest_all, w_query, w_key, w_value, ext_rest,
        HEADS // 2, q_rows, (attn_main,))
    grad_moved = to_groups(cotangent, (attn_main,))
    grad_low = jnp.concatenate([hold(g, (attn_rest,)) for g in grad_moved] + [cotangent[GROUPS]], axis=0)

    def swap_in(array):
        pieces = []
        for step in range(members):
            part = array[step * main_own:(step + 1) * main_own, :mine_cols]
            pieces.append(part if step == 0 else lax.ppermute(part, "seq", member_perm(step)))
        out = jnp.zeros((main_own, width), array.dtype)
        for step in range(members):
            out = lax.dynamic_update_slice_in_dim(out, pieces[step], slot_of(member ^ step) * mine_cols, 1)
        return out

    attn_in = jnp.concatenate([swap_in(attn_main), attn_rest], axis=0)
    resid = jnp.concatenate([main_rows, rest_f32], axis=0)
    branch_one = dot(attn_in, w_out)
    middle = resid + branch_one
    second_in = (middle * norm_scale(middle) * gain_two).astype(BF)
    ff_ins = (second_in, grad_low, w_gate, w_up, w_down)
    sums_two, sums_gs, ff_sent = ff_half(there, *ff_ins, None)
    branch_two, grad_second, ff_kept = ff_half(here_place, *ff_ins, (sums_two, sums_gs))
    ff_now = add_low(ff_kept, core_move(ff_sent))
    img_fours = [list(range(i, i + 4)) for i in range(0, n_img, 4)]
    same_member = [[g * members + r for g in range(GROUPS)] for r in range(members)]
    ff_quarter = lax.psum_scatter(ff_now, "img", scatter_dimension=0, axis_index_groups=img_fours)
    branch_two = hold(branch_two, (ff_now,))
    result = middle + branch_two
    squares = jnp.stack([masked_squares(v, row_mask) for v in (resid, branch_one, branch_two, result)])
    valid_count = jnp.sum(row_mask)
    result_low = result.astype(BF)
    layer_out = from_groups(result_low)
    grad_out = grad_low.astype(F32)
    grad_second = hold(grad_second, (ff_now,))
    grad_mid_norm, grad_gain_two = norm_back(middle, gain_two, grad_second)
    grad_mid = grad_out + grad_mid_norm
    grad_mid_low = grad_mid.astype(BF)

    main_grads = []
    for step in range(members):
        rows_of = lax.dynamic_slice_in_dim(w_out, slot_of(member ^ step) * mine_cols, mine_cols, 0)
        part = dot_nt(grad_mid_low[:main_own], rows_of).astype(BF)
        if pad_cols:
            part = jnp.pad(part, ((0, 0), (0, pad_cols)))
        main_grads.append(part if step == 0 else lax.ppermute(part, "seq", member_perm(step)))
    grad_attn_main = jnp.concatenate(main_grads, axis=0)
    grad_attn_rest = dot_nt(grad_mid_low[main_own:], w_out).astype(BF)

    dq_rest, dk_rest, dv_rest = attend_back(
        query_rest, key_rest, value_rest, ext_rest, logs_rest, attn_rest, grad_attn_rest, q_rows)
    first_part_rest = (dot_nt(dk_rest, w_key) + dot_nt(dv_rest, w_value)).astype(BF)
    by_owner = first_part_rest.reshape(GROUPS, members, block_len, width)
    first_sum_rest = lax.dynamic_index_in_dim(by_owner, member, 1, keepdims=False).astype(F32)
    for step in range(1, members):
        part = lax.dynamic_index_in_dim(by_owner, member ^ step, 1, keepdims=False)
        first_sum_rest = first_sum_rest + lax.ppermute(part, "seq", member_perm(step)).astype(F32)
    by_owner = first_sum_rest.astype(BF)
    first_sum_rest = lax.dynamic_index_in_dim(by_owner, group, 0, keepdims=False).astype(F32)
    for step in range(1, GROUPS):
        part = lax.dynamic_index_in_dim(by_owner, group ^ step, 0, keepdims=False)
        first_sum_rest = first_sum_rest + z_move(part, step).astype(F32)
    half_width = width // 2
    rest_ins = [(first_rest, False), (dq_rest, True), (first_rest_all, False), (dk_rest, True),
                (dv_rest, True), (attn_in, False), (grad_mid_low, True)]
    qkv_sent = grad_part(there, rest_ins, [
        (0, 0, [(0, 1)]), (0, half_width, [(5, 6)]), (1, 0, [(2, 3)]), (1, half_width, [(2, 4)])],
        (first_part_rest,))
    dq_main, dk_main, dv_main = attend_back(
        query_main, key_main, value_main, ext_main, logs_main, attn_main, grad_attn_main,
        min(256, block_len * 2), (qkv_sent, layer_out))

    main_parts = [(dq_main, w_query), (dk_main, w_key), (dv_main, w_value)]
    def in_half(part):
        part = part[:, :mine_cols]
        if mine_cols == width // 2:
            return part
        empty = jnp.zeros((part.shape[0], width // 2), part.dtype)
        return lax.dynamic_update_slice_in_dim(empty, part, (member // 2) * mine_cols, 1)

    main_ins = [(first_all, False), (in_half(dq_main), False), (in_half(dk_main), False),
                (in_half(dv_main), False)]
    qkv_kept = grad_part(here_place, rest_ins + main_ins, [
        (0, 0, [(0, 1), (7, 8)]), (0, half_width, [(5, 6)]),
        (1, 0, [(2, 3), (7, 9)]), (1, half_width, [(2, 4), (7, 10)])])
    qkv_now = split_cores(here_place, qkv_kept, core_move(qkv_sent))
    main_parts = [(hold(part, qkv_now), w) for part, w in main_parts]
    first_part_main = sum(
        dot_nt(part[:, :mine_cols], lax.dynamic_slice_in_dim(w, slot_of(member) * mine_cols, mine_cols, 1))
        for part, w in main_parts)
    grad_first_main = first_part_main[:main_own]
    for step in range(1, members):
        part = first_part_main[step * main_own:(step + 1) * main_own].astype(BF)
        grad_first_main = grad_first_main + lax.ppermute(part, "seq", member_perm(step)).astype(F32)
    grad_first_rest = dot_nt(dq_rest, w_query) + first_sum_rest
    grad_first = jnp.concatenate([grad_first_main, grad_first_rest], axis=0)

    qkv_now = sum_img_first(*qkv_now)
    ff_quarter = hold(ff_quarter, (dq_main,))
    ff_shard = lax.psum_scatter(ff_quarter, "seq", scatter_dimension=0, axis_index_groups=same_member)
    for move in more_moves:
        ff_shard = add_low(ff_shard, move(ff_shard))
    ff_shard = hold(ff_shard, (first_part_main,))
    ff_groups = lax.all_gather(ff_shard, "seq", axis=0, axis_index_groups=same_member)
    grad_resid_norm, grad_gain_one = norm_back(resid, gain_one, grad_first)
    grad_input_rows = (grad_mid + grad_resid_norm).astype(BF)
    grad_input = from_groups(grad_input_rows)
    qkv_now = sum_img_second(*qkv_now)
    ff_groups = hold(ff_groups, qkv_now)
    ff_own = lax.all_gather(ff_groups, "img", axis=0, axis_index_groups=img_fours)
    qkv_near = halves(quarters(sum_groups(qkv_now), ()), (grad_input,))
    ff_own = hold(ff_own, qkv_near)
    sum_gate, sum_up, sum_down = assemble_ff(here_place, ff_own, core_move(ff_own), w_gate.shape[1])
    sum_query, sum_out, sum_key, sum_value = assemble(
        assemble_kernel, here_place, every_piece(qkv_near, far_halves(qkv_near, ())), [(width, width)] * 4,
        [pl.BlockSpec((width // 4, width), lambda q, p: (q, 0))] * 4)

    small = jnp.concatenate([grad_gain_one, grad_gain_two, squares, valid_count[None]])
    small = jnp.pad(small, (0, -small.size % 1024)).reshape(-1, 128)
    for move in z_moves + [core_move] + img_moves + more_moves:
        small = small + move(small)
    small = small.reshape(-1)
    sum_gain_one, sum_gain_two = small[:width], small[width:2 * width]
    sum_squares, sum_count = small[2 * width:2 * width + 4], small[2 * width + 4]
    rms_stats = jnp.sqrt(sum_squares / (sum_count * width))
    return (layer_out, grad_input, sum_gain_one, sum_query, sum_key, sum_value, sum_out,
            sum_gain_two, sum_gate, sum_up, sum_down, rms_stats)


def solution(mesh):
    rows = P("img", "seq", None)
    return jax.shard_map(
        functools.partial(body, mesh.shape["img"], mesh.shape["seq"]),
        mesh=mesh,
        in_specs=(rows, P("img"), P(), P(), P(), P(), P(), P(), P(), P(), P(), rows),
        out_specs=(rows, rows, P(), P(), P(), P(), P(), P(), P(), P(), P(), P()),
        check_vma=False,
    )
```

time: 520 us -> 411 us (0.79)
  waiting for transfers between devices: 217 us -> 87.1 us
  Pallas kernels: 65 us -> 152 us
  blocking collectives: 48.2 us -> 0 us
  matrix products: 65.1 us -> 22.4 us
  starting transfers between devices: 22.5 us -> 56.1 us
  other arithmetic: 53.8 us -> 34.9 us
  local copies, waits for them, and re-layouts: 29.4 us -> 36.3 us
    psum x1 -> x0, waiting for transfers between devices: 197 us -> none  [total(): return lax.psum(tuple((a.astype(BF) for a in arrays)), ('img', 'seq'))]
    pallas_call x0 -> x30, Pallas kernels: none -> 96.6 us  [the longest x2 36.2 us: ff_half(): pl.pallas_call(functools.partial(ff_kernel, sums is None), grid_spec=pltp...]
    ppermute x6 -> x35, waiting for transfers between devices: 19.2 us -> 72.7 us  [the longest x20 35.9 us: move(): return lax.ppermute(array, 'img' if axis == 'img' else 'seq', perm)]
    psum x1 -> x0, blocking collectives: 48.2 us -> none  [body(): lax.psum((grad_gain_one, grad_gain_two, squares, valid_count), ('img', 's...]
    ppermute x6 -> x35, starting transfers between devices: 10.8 us -> 45.6 us  [the longest x9 18.8 us: z_move(): return lax.ppermute(array, 'seq', perm)]
    dot_general x10 -> x0, matrix products: 25.9 us -> none  [dot_tn(): lax.dot_general(left, right, (((0,), (0,)), ((), ())), preferred_element_...]
    ppermute x6, waiting for transfers between devices: 0.02 us -> 14.3 us  [from_groups(): lax.ppermute(part, 'seq', shift_perm(-step))]
    convert_element_type x10 -> x3, other arithmetic: 22.1 us -> 8.46 us  [the longest x1 6 us: add_low(): return (left.astype(F32) + right.astype(F32)).astype(BF)]
  transfers between devices with their start and end apart: 19 -> 51, of which waited for: 4 -> 20; matrix products, arithmetic and copies ran while one was open for 16% -> 15% of each run, Pallas kernels for 10% -> 31%
where the time goes in v2:
time: 411 us; the launch traced here: 405 us
  Pallas kernels  152 us (37%)
  waiting for transfers between devices  87.1 us (21%)
  starting transfers between devices  56.1 us (14%)
  local copies, waits for them, and re-layouts  36.3 us (9%)
  other arithmetic  34.9 us (8%)
  matrix products  22.4 us (5%)
  between operations  15.6 us (4%)
    pallas_call x2, Pallas kernels, ff_half(): pl.pallas_call(functools.partial(ff_kernel, sums is None), grid_spec=pltp...  36.2 us
    ppermute x20, waiting for transfers between devices, move(): return lax.ppermute(array, 'img' if axis == 'img' else 'seq', perm)  35.9 us
    pallas_call x2, Pallas kernels, attend(): pl.pallas_call(functools.partial(attend_kernel, q_rows), grid_spec=pltpu....  27.9 us
    pallas_call x2, Pallas kernels, attend_back(): pl.pallas_call(functools.partial(attend_back_kernel, q_rows), grid=(pairs...  27.7 us
    ppermute x9, waiting for transfers between devices, z_move(): return lax.ppermute(array, 'seq', perm)  24.4 us
    unnamed x142, local copies, waits for them, and re-layouts  22.8 us
    dot_general x9, matrix products, dot_nt(): lax.dot_general(left, right, (((1,), (1,)), ((), ())), preferred_element_...  18.9 us
    ppermute x9, starting transfers between devices, z_move(): return lax.ppermute(array, 'seq', perm)  18.8 us
  transfers between devices with their start and end apart: 51, of which 20 were waited for; matrix products, arithmetic and copies ran while one was open for 15% of the time, Pallas kernels for 31%

profile of v2, /device:TPU:0, one launch (start us, length us, event | category | flops | bytes accessed | tf_op | source)
XLA Modules:
  0.0 404.6 jit_solution(13831727782480390684)
XLA Ops:
  7.4 2.1 bitcast_convert_fusion
  9.5 3.0 collective-permute-start
  12.5 2.6 collective-permute-start.1
  20.4 7.6 %collective-permute-done.1 = bf16[128,768]{1,0:T(8,128)(2,1)S(1)} collective-permute-done((bf16[128,768]{1,0:T(8,128)(2,1)S(1)}, bf16[128,768]{1,0:T(8,128)(2,1)S(1)}, u32[]{:S(2)}, u32[]{:S(2)}) %collective-permute-start.1) | collective-permute-done | bytes 196640 | tf_op jit(solution)/shard_map/ppermute | solution.py:666
  32.5 15.2 %shard_map.211 = (bf16[3,1024,128]{2,1,0:T(8,128)(2,1)}, bf16[3,1024,128]{2,1,0:T(8,128)(2,1)}, bf16[3,1024,128]{2,1,0:T(8,128)(2,1)}, bf16[6,1024,128]{2,1,0:T(8,128)(2,1)}, bf16[1024,384]{1,0:T(8,128)(2,1)}) custom-call(s32[1]{0:T(128)} %bitcast.9.place_ref, bf16[1024,768]{1,0:T(8,128)(2,1)} %pad_maximum_fusion.2.fiq_ref.fik_ref.refs_7_, ...), custom_call_target="tpu_custom_call" | custom-call | flops 10066329600 | bytes 12582912 | tf_op jit(solution)/shard_map/pallas_call | solution.py:96
  52.4 5.7 %collective-permute-start.7 = (bf16[128,768]{1,0:T(8,128)(2,1)}, bf16[128,768]{1,0:T(8,128)(2,1)S(1)}, u32[]{:S(2)}, u32[]{:S(2)}) collective-permute-start(bf16[128,768]{1,0:T(8,128)(2,1)} %shard_map.218), channel_id=1, source_target_pairs={{0,6},{1,7},{2,0},{3,1},{4,2},{5,3},{6,4},{7,5},{8,14},{9,15},{10,... | collective-permute-start | bytes 589832 | tf_op jit(solution)/shard_map/ppermute | solution.py:666
  59.0 12.7 %shard_map.212 = (bf16[6,128,128]{2,1,0:T(8,128)(2,1)}, bf16[6,1024,128]{2,1,0:T(8,128)(2,1)}, bf16[6,1024,128]{2,1,0:T(8,128)(2,1)}, bf16[12,128,128]{2,1,0:T(8,128)(2,1)}, bf16[128,768]{1,0:T(8,128)(2,1)}) custom-call(s32[1]{0:T(128)} %constant.214.clone.1.place_ref, bf16[128,768]{1,0:T(8,128)(2,1)} %multiply_convert_fusion.2.fiq_ref.refs_0_, ...), custom_call_target="tpu_custom_call" | custom-call | flops 6744440832 | bytes 7077888 | tf_op jit(solution)/shard_map/pallas_call | solution.py:96
  71.7 4.5 %collective-permute-done.6.refs_0_ = bf16[128,768]{1,0:T(8,128)(2,1)S(1)} collective-permute-done((bf16[128,768]{1,0:T(8,128)(2,1)}, bf16[128,768]{1,0:T(8,128)(2,1)S(1)}, u32[]{:S(2)}, u32[]{:S(2)}) %collective-permute-start.6) | collective-permute-done | bytes 196640 | tf_op jit(solution)/shard_map/ppermute | solution.py:666
  84.0 3.5 multiply_reduce_fusion.8
  88.9 17.5 %shard_map.220 = (f32[640,768]{1,0:T(8,128)}, f32[640,768]{1,0:T(8,128)}, bf16[4,4,576,256]{3,2,1,0:T(8,128)(2,1)}) custom-call(s32[4]{0:T(128)} %get-tuple-element.154.place_ref, bf16[640,768]{1,0:T(8,128)(2,1)} %multiply_convert_fusion.second_ref, bf16[640,768]{1,0:T(8,128)(2,1)} %copy-done.17, bf16[768,2048]{1,0:T(8,128)(2,1)} %wg_ref.3, ...), custom_call_target="tpu_custom_call" | custom-call | flops 9059696640 | bytes 17301504 | tf_op jit(solution)/shard_map/pallas_call | solution.py:255
  106.4 18.7 %shard_map.221 = (f32[640,768]{1,0:T(8,128)}, f32[640,768]{1,0:T(8,128)}, bf16[4,4,576,256]{3,2,1,0:T(8,128)(2,1)}) custom-call(s32[4]{0:T(128)} %get-tuple-element.153.place_ref, bf16[640,768]{1,0:T(8,128)(2,1)} %multiply_convert_fusion.second_ref, bf16[640,768]{1,0:T(8,128)(2,1)} %copy-done.17, bf16[768,2048]{1,0:T(8,128)(2,1)} %wg_ref.3, ...), custom_call_target="tpu_custom_call" | custom-call | flops 9059696640 | bytes 17301504 | tf_op jit(solution)/shard_map/pallas_call | solution.py:255
  125.1 6.0 %add_convert_fusion.refs_1_ = bf16[4,4,576,256]{3,2,1,0:T(8,128)(2,1)} fusion(bf16[4,4,576,256]{3,2,1,0:T(8,128)(2,1)S(1)} %collective-permute-done.8, bf16[4,4,576,256]{3,2,1,0:T(8,128)(2,1)} %get-tuple-element.64), kind=kLoop, calls=%fused_computation | loop fusion | flops 9437184 | bytes 14155776 | tf_op jit(solution)/shard_map/convert_element_type | solution.py:560
  131.2 2.1 pad_maximum_fusion.3.refs_5_
  133.4 3.8 multiply_reduce_fusion
  140.5 4.0 collective-permute-start.9
  145.7 8.5 %shard_map.225 = (bf16[128,768]{1,0:T(8,128)(2,1)}, bf16[1024,768]{1,0:T(8,128)(2,1)}, bf16[1024,768]{1,0:T(8,128)(2,1)}) custom-call(bf16[6,128,128]{2,1,0:T(8,128)(2,1)} %get-tuple-element.71.q_ref, bf16[6,1024,128]{2,1,0:T(8,128)(2,1)} %get-tuple-element.72.k_ref, bf16[6,1024,128]{2,1,0:T(8,128)(2,1)} %get-tuple-element.73.v_ref, ...), custom_call_target="tpu_custom_call" | custom-call | flops 2013265920 | bytes 7077888 | tf_op jit(solution)/shard_map/pallas_call | solution.py:168
  154.2 3.0 fusion.36
  157.2 2.7 add_convert_fusion.1.refs_7_
  159.9 7.2 %shard_map.226.refs_0_ = bf16[2,4,4,48,768]{4,3,2,1,0:T(8,128)(2,1)} custom-call(s32[4]{0:T(128)} %get-tuple-element.154.place_ref, bf16[128,768]{1,0:T(8,128)(2,1)} %multiply_convert_fusion.2.fiq_ref.refs_0_, bf16[128,768]{1,0:T(8,128)(2,1)} %get-tuple-element.75.refs_1_, bf16[1024,768]{1,0:T(8,128)(2,1)} %all-gather.6.cloned.1.call-done.fik_ref.refs_2_, ...), custom_call_target="tpu_custom_call" | custom-call | flops 1660944384 | bytes 7077888 | tf_op jit(solution)/shard_map/pallas_call | solution.py:456
  168.5 3.3 shard_map.223.refs_1_
  173.8 19.2 %shard_map.227 = (bf16[1024,384]{1,0:T(8,128)(2,1)}, bf16[1024,384]{1,0:T(8,128)(2,1)}, bf16[1024,384]{1,0:T(8,128)(2,1)}) custom-call(bf16[3,1024,128]{2,1,0:T(8,128)(2,1)} %get-tuple-element.67.q_ref, bf16[3,1024,128]{2,1,0:T(8,128)(2,1)} %get-tuple-element.68.k_ref, bf16[3,1024,128]{2,1,0:T(8,128)(2,1)} %get-tuple-element.69.v_ref, ...), custom_call_target="tpu_custom_call" | custom-call | flops 8053063680 | bytes 6291456 | tf_op jit(solution)/shard_map/pallas_call | solution.py:168
  193.5 10.6 %shard_map.228.refs_0_.refs_1_.refs_2_.refs_3_ = bf16[2,4,4,48,768]{4,3,2,1,0:T(8,128)(2,1)} custom-call(s32[4]{0:T(128)} %get-tuple-element.153.place_ref, bf16[128,768]{1,0:T(8,128)(2,1)} %multiply_convert_fusion.2.fiq_ref.refs_0_, bf16[128,768]{1,0:T(8,128)(2,1)} %get-tuple-element.75.refs_1_, ...), custom_call_target="tpu_custom_call" | custom-call | flops 3472883712 | bytes 11010048 | tf_op jit(solution)/shard_map/pallas_call | solution.py:456
  205.5 4.3 %shard_map.229 = (bf16[2,4,48,768]{3,2,1,0:T(8,128)(2,1)}, bf16[2,4,48,768]{3,2,1,0:T(8,128)(2,1)}, bf16[2,4,48,768]{3,2,1,0:T(8,128)(2,1)}, bf16[2,4,48,768]{3,2,1,0:T(8,128)(2,1)}) custom-call(s32[4]{0:T(128)} %get-tuple-element.153.place_ref, bf16[2,4,4,48,768]{4,3,2,1,0:T(8,128)(2,1)} %shard_map.228.refs_0_.refs_1_.refs_2_.refs_3_, ...), custom_call_target="tpu_custom_call" | custom-call | bytes 7077888 | tf_op jit(solution)/shard_map/pallas_call | solution.py:297
  211.1 3.8 fusion.7
  216.1 2.3 fusion.9
  218.9 2.7 add_add_fusion.refs_1_
  225.4 13.1 %collective-permute-done.27.rx_ref = bf16[2,4,48,768]{3,2,1,0:T(8,128)(2,1)S(1)} collective-permute-done((bf16[2,4,48,768]{3,2,1,0:T(8,128)(2,1)S(1)}, bf16[2,4,48,768]{3,2,1,0:T(8,128)(2,1)S(1)}, u32[]{:S(2)}, u32[]{:S(2)}) %collective-permute-start.27) | collective-permute-done | bytes 589856 | tf_op jit(solution)/shard_map/ppermute | solution.py:606
  240.3 3.7 shard_map.234
  246.6 6.3 %collective-permute-done.29.rx_ref = bf16[4,48,768]{2,1,0:T(8,128)(2,1)S(1)} collective-permute-done((bf16[4,48,768]{2,1,0:T(8,128)(2,1)}, bf16[4,48,768]{2,1,0:T(8,128)(2,1)S(1)}, u32[]{:S(2)}, u32[]{:S(2)}) %collective-permute-start.29) | collective-permute-done | bytes 294944 | tf_op jit(solution)/shard_map/ppermute | solution.py:606
  254.7 2.1 shard_map.235
  262.2 2.5 slice.138
  268.2 2.1 collective-permute-start.17
  271.7 3.0 collective-permute-start.33
  275.4 11.7 %collective-permute-done.33.refs_3_ = bf16[2,48,768]{2,1,0:T(8,128)(2,1)S(1)} collective-permute-done((bf16[2,48,768]{2,1,0:T(8,128)(2,1)S(1)}, bf16[2,48,768]{2,1,0:T(8,128)(2,1)S(1)}, u32[]{:S(2)}, u32[]{:S(2)}) %collective-permute-start.33) | collective-permute-done | bytes 147488 | tf_op jit(solution)/shard_map/ppermute | solution.py:614
  289.6 8.5 %collective-permute-start.34 = (bf16[2,48,768]{2,1,0:T(8,128)(2,1)}, bf16[2,48,768]{2,1,0:T(8,128)(2,1)S(1)}, u32[]{:S(2)}, u32[]{:S(2)}) collective-permute-start(bf16[2,48,768]{2,1,0:T(8,128)(2,1)} %shard_map.236.refs_0_), channel_id=1, source_target_pairs={{0,2},{1,3},{2,0},{3,1},{4,6},{5,7},{6,4},{7,5},{8,10},{9,11},{10,... | collective-permute-start | bytes 442376 | tf_op jit(solution)/shard_map/ppermute | solution.py:614
  300.7 2.8 collective-permute-done.34.refs_1_
  303.5 8.4 %collective-permute-done.35.refs_2_ = bf16[2,48,768]{2,1,0:T(8,128)(2,1)S(1)} collective-permute-done((bf16[2,48,768]{2,1,0:T(8,128)(2,1)}, bf16[2,48,768]{2,1,0:T(8,128)(2,1)S(1)}, u32[]{:S(2)}, u32[]{:S(2)}) %collective-permute-start.35) | collective-permute-done | bytes 147488 | tf_op jit(solution)/shard_map/ppermute | solution.py:614
  327.8 2.7 collective-permute-done.19.refs_1_
  330.5 11.5 %collective-permute-done.20.refs_2_ = bf16[128,768]{1,0:T(8,128)(2,1)S(1)} collective-permute-done((bf16[128,768]{1,0:T(8,128)(2,1)S(1)}, bf16[128,768]{1,0:T(8,128)(2,1)S(1)}, u32[]{:S(2)}, u32[]{:S(2)}) %collective-permute-start.20) | collective-permute-done | bytes 196640 | tf_op jit(solution)/shard_map/ppermute | solution.py:674
  342.8 3.0 shard_map.233.refs_0_
  347.2 3.5 shard_map.238
  351.3 3.3 concatenate.43
  357.0 3.6 collective-permute-done.22
  360.7 4.5 %collective-permute-done.23 = f32[16,128]{1,0:T(8,128)S(1)} collective-permute-done((f32[16,128]{1,0:T(8,128)S(1)}, f32[16,128]{1,0:T(8,128)S(1)}, u32[]{:S(2)}, u32[]{:S(2)}) %collective-permute-start.23) | collective-permute-done | bytes 8224 | tf_op jit(solution)/shard_map/ppermute | solution.py:606
  367.7 2.3 collective-permute-done.25
  371.6 2.1 collective-permute-done.26
  378.8 8.0 %shard_map.239 = (f32[768,768]{1,0:T(8,128)}, f32[768,768]{1,0:T(8,128)}, f32[768,768]{1,0:T(8,128)}, f32[768,768]{1,0:T(8,128)}) custom-call(s32[4]{0:T(128)} %get-tuple-element.153.place_ref, bf16[2,4,48,768]{3,2,1,0:T(8,128)(2,1)} %get-tuple-element.95.refs_0_.refs_1_, bf16[2,4,48,768]{3,2,1,0:T(8,128)(2,1)} %copy-done.31, ...), custom_call_target="tpu_custom_call" | custom-call | bytes 9437184 | tf_op jit(solution)/shard_map/pallas_call | solution.py:547
  386.9 11.0 %shard_map.244 = (f32[768,2048]{1,0:T(8,128)}, f32[768,2048]{1,0:T(8,128)}, f32[4,4,128,768]{3,2,1,0:T(8,128)}) custom-call(s32[4]{0:T(128)} %get-tuple-element.153.place_ref, bf16[4,4,576,256]{3,2,1,0:T(8,128)(2,1)} %shard_map.243.own_ref, bf16[4,4,576,256]{3,2,1,0:T(8,128)(2,1)} %collective-permute-done.45.other_ref), custom_call_target="tpu_custom_call" | custom-call | bytes 28311552 | tf_op jit(solution)/shard_map/pallas_call | solution.py:516
  (302 shorter events, 92.7 us)
Async XLA Ops:
  7.2 51.7 %all-gather.6.cloned.1.call-start = ((), (), s32[]{:S(2)}) async-start(), calls=%async_computation.2 | async-start | bytes 1769472 | tf_op jit(solution)/shard_map/all_gather | solution.py:718
  9.5 10.9 %collective-permute-start = (bf16[128,768]{1,0:T(8,128)(2,1)S(1)}, bf16[128,768]{1,0:T(8,128)(2,1)S(1)}, u32[]{:S(2)}, u32[]{:S(2)}) collective-permute-start(bf16[128,768]{1,0:T(8,128)(2,1)S(1)} %get-tuple-element.138), channel_id=1, source_target_pairs={{0,2},{1,3},{2,4},{3,5},{4,6},{5,7},{6,0},{7,1},{8,10},{9,11},{10,... | collective-permute-start | bytes 589832 | tf_op jit(solution)/shard_map/ppermute | solution.py:666
  12.5 15.5 %collective-permute-start.1 = (bf16[128,768]{1,0:T(8,128)(2,1)S(1)}, bf16[128,768]{1,0:T(8,128)(2,1)S(1)}, u32[]{:S(2)}, u32[]{:S(2)}) collective-permute-start(bf16[128,768]{1,0:T(8,128)(2,1)S(1)} %get-tuple-element.137), channel_id=1, source_target_pairs={{0,4},{1,5},{2,6},{3,7},{4,0},{5,1},{6,2},{7,3},{8,12},{9,13},{10,... | collective-permute-start | bytes 589832 | tf_op jit(solution)/shard_map/ppermute | solution.py:666
  15.1 12.9 %collective-permute-start.2 = (bf16[128,768]{1,0:T(8,128)(2,1)S(1)}, bf16[128,768]{1,0:T(8,128)(2,1)S(1)}, u32[]{:S(2)}, u32[]{:S(2)}) collective-permute-start(bf16[128,768]{1,0:T(8,128)(2,1)S(1)} %get-tuple-element.140), channel_id=1, source_target_pairs={{0,6},{1,7},{2,0},{3,1},{4,2},{5,3},{6,4},{7,5},{8,14},{9,15},{10,... | collective-permute-start | bytes 589832 | tf_op jit(solution)/shard_map/ppermute | solution.py:666
  28.5 164.5 %reduce-scatter.7.cloned.1.call-start = ((), (), s32[]{:S(2)}) async-start(), calls=%async_computation.6 | async-start | bytes 5898240
  49.1 9.8 %collective-permute-start.4 = (bf16[512,384]{1,0:T(8,128)(2,1)S(1)}, bf16[512,384]{1,0:T(8,128)(2,1)S(1)}, u32[]{:S(2)}, u32[]{:S(2)}) collective-permute-start(bf16[512,384]{1,0:T(8,128)(2,1)S(1)} %get-tuple-element.144), channel_id=1, source_target_pairs={{0,1},{1,0},{2,3},{3,2},{4,5},{5,4},{6,7},{7,6},{8,9},{9,8},{10,11... | collective-permute-start | bytes 1179656 | tf_op jit(solution)/shard_map/ppermute | solution.py:741
  52.4 28.0 %collective-permute-start.7 = (bf16[128,768]{1,0:T(8,128)(2,1)}, bf16[128,768]{1,0:T(8,128)(2,1)S(1)}, u32[]{:S(2)}, u32[]{:S(2)}) collective-permute-start(bf16[128,768]{1,0:T(8,128)(2,1)} %shard_map.218), channel_id=1, source_target_pairs={{0,6},{1,7},{2,0},{3,1},{4,2},{5,3},{6,4},{7,5},{8,14},{9,15},{10,... | collective-permute-start | bytes 589832 | tf_op jit(solution)/shard_map/ppermute | solution.py:666
  58.1 18.1 %collective-permute-start.6 = (bf16[128,768]{1,0:T(8,128)(2,1)}, bf16[128,768]{1,0:T(8,128)(2,1)S(1)}, u32[]{:S(2)}, u32[]{:S(2)}) collective-permute-start(bf16[128,768]{1,0:T(8,128)(2,1)} %shard_map.216), channel_id=1, source_target_pairs={{0,4},{1,5},{2,6},{3,7},{4,0},{5,1},{6,2},{7,3},{8,12},{9,13},{10,... | collective-permute-start | bytes 589832 | tf_op jit(solution)/shard_map/ppermute | solution.py:666
  58.5 19.3 %collective-permute-start.5 = (bf16[128,768]{1,0:T(8,128)(2,1)}, bf16[128,768]{1,0:T(8,128)(2,1)S(1)}, u32[]{:S(2)}, u32[]{:S(2)}) collective-permute-start(bf16[128,768]{1,0:T(8,128)(2,1)} %shard_map.214), channel_id=1, source_target_pairs={{0,2},{1,3},{2,4},{3,5},{4,6},{5,7},{6,0},{7,1},{8,10},{9,11},{10,... | collective-permute-start | bytes 589832 | tf_op jit(solution)/shard_map/ppermute | solution.py:666
  106.4 18.7 %collective-permute-start.8 = (bf16[4,4,576,256]{3,2,1,0:T(8,128)(2,1)}, bf16[4,4,576,256]{3,2,1,0:T(8,128)(2,1)S(1)}, u32[]{:S(2)}, u32[]{:S(2)}) collective-permute-start(bf16[4,4,576,256]{3,2,1,0:T(8,128)(2,1)} %get-tuple-element.65), channel_id=1, source_target_pairs={{0,1},{1,0},{2,3},{3,2},{4,5},{5,4},{6,7},{7,6},{8,9},{9,8},{10,11... | collective-permute-start | bytes 14155784 | tf_op jit(solution)/shard_map/ppermute | solution.py:606
  131.2 90.4 %reduce-scatter.5.cloned.1.call-start = ((), (), s32[]{:S(2)}) async-start(), calls=%async_computation.3 | async-start | bytes 1474560 | tf_op jit(solution)/shard_map/reduce_scatter | solution.py:831
  139.1 32.7 %collective-permute-start.12 = (bf16[512,384]{1,0:T(8,128)(2,1)}, bf16[512,384]{1,0:T(8,128)(2,1)}, u32[]{:S(2)}, u32[]{:S(2)}) collective-permute-start(bf16[512,384]{1,0:T(8,128)(2,1)} %convolution_convert_fusion), channel_id=1, source_target_pairs={{0,1},{1,0},{2,3},{3,2},{4,5},{5,4},{6,7},{7,6},{8,9},{9,8},{10,11... | collective-permute-start | bytes 1179656 | tf_op jit(solution)/shard_map/ppermute | solution.py:777
  140.4 28.1 %collective-permute-start.10 = (bf16[128,768]{1,0:T(8,128)(2,1)S(1)}, bf16[128,768]{1,0:T(8,128)(2,1)}, u32[]{:S(2)}, u32[]{:S(2)}) collective-permute-start(bf16[128,768]{1,0:T(8,128)(2,1)S(1)} %get-tuple-element.129), channel_id=1, source_target_pairs={{0,4},{1,5},{2,6},{3,7},{4,0},{5,1},{6,2},{7,3},{8,12},{9,13},{10,... | collective-permute-start | bytes 589832 | tf_op jit(solution)/shard_map/ppermute | solution.py:674
  140.5 28.0 %collective-permute-start.11 = (bf16[128,768]{1,0:T(8,128)(2,1)S(1)}, bf16[128,768]{1,0:T(8,128)(2,1)}, u32[]{:S(2)}, u32[]{:S(2)}) collective-permute-start(bf16[128,768]{1,0:T(8,128)(2,1)S(1)} %get-tuple-element.128), channel_id=1, source_target_pairs={{0,2},{1,3},{2,4},{3,5},{4,6},{5,7},{6,0},{7,1},{8,10},{9,11},{10,... | collective-permute-start | bytes 589832 | tf_op jit(solution)/shard_map/ppermute | solution.py:674
  140.5 28.0 %collective-permute-start.9 = (bf16[128,768]{1,0:T(8,128)(2,1)S(1)}, bf16[128,768]{1,0:T(8,128)(2,1)}, u32[]{:S(2)}, u32[]{:S(2)}) collective-permute-start(bf16[128,768]{1,0:T(8,128)(2,1)S(1)} %get-tuple-element.130), channel_id=1, source_target_pairs={{0,6},{1,7},{2,0},{3,1},{4,2},{5,3},{6,4},{7,5},{8,14},{9,15},{10,... | collective-permute-start | bytes 589832 | tf_op jit(solution)/shard_map/ppermute | solution.py:674
  167.1 37.0 %collective-permute-start.13 = (bf16[2,4,4,48,768]{4,3,2,1,0:T(8,128)(2,1)}, bf16[2,4,4,48,768]{4,3,2,1,0:T(8,128)(2,1)S(1)}, u32[]{:S(2)}, u32[]{:S(2)}) collective-permute-start(bf16[2,4,4,48,768]{4,3,2,1,0:T(8,128)(2,1)} %shard_map.226.refs_0_), channel_id=1, source_target_pairs={{0,1},{1,0},{2,3},{3,2},{4,5},{5,4},{6,7},{7,6},{8,9},{9,8},{10,11... | collective-permute-start | bytes 7077896 | tf_op jit(solution)/shard_map/ppermute | solution.py:606
  193.1 63.7 %all-gather.8.cloned.1.call-start = ((), (), s32[]{:S(2)}) async-start(), calls=%async_computation.4 | async-start | bytes 1474560 | tf_op jit(solution)/shard_map/all_gather | solution.py:835
  221.6 129.1 %all-gather.10.cloned.1.call-start = ((), (), s32[]{:S(2)}) async-start(), calls=%async_computation.5 | async-start | bytes 5898240 | tf_op jit(solution)/shard_map/all_gather | solution.py:841
  222.6 15.9 %collective-permute-start.27 = (bf16[2,4,48,768]{3,2,1,0:T(8,128)(2,1)S(1)}, bf16[2,4,48,768]{3,2,1,0:T(8,128)(2,1)S(1)}, u32[]{:S(2)}, u32[]{:S(2)}) collective-permute-start(bf16[2,4,48,768]{3,2,1,0:T(8,128)(2,1)S(1)} %copy-done.15), channel_id=1, source_target_pairs={{0,8},{8,0},{16,24},{24,16},{1,9},{9,1},{17,25},{25,17},{2,10},{10... | collective-permute-start | bytes 1769480 | tf_op jit(solution)/shard_map/ppermute | solution.py:606
  223.9 15.6 %collective-permute-start.28 = (bf16[2,4,48,768]{3,2,1,0:T(8,128)(2,1)S(1)}, bf16[2,4,48,768]{3,2,1,0:T(8,128)(2,1)S(1)}, u32[]{:S(2)}, u32[]{:S(2)}) collective-permute-start(bf16[2,4,48,768]{3,2,1,0:T(8,128)(2,1)S(1)} %copy-done.14), channel_id=1, source_target_pairs={{0,16},{8,24},{16,0},{24,8},{1,17},{9,25},{17,1},{25,9},{2,18},{10... | collective-permute-start | bytes 1769480 | tf_op jit(solution)/shard_map/ppermute | solution.py:606
  244.0 8.9 %collective-permute-start.29 = (bf16[4,48,768]{2,1,0:T(8,128)(2,1)}, bf16[4,48,768]{2,1,0:T(8,128)(2,1)S(1)}, u32[]{:S(2)}, u32[]{:S(2)}) collective-permute-start(bf16[4,48,768]{2,1,0:T(8,128)(2,1)} %get-tuple-element.86), channel_id=1, source_target_pairs={{0,16},{8,24},{16,0},{24,8},{1,17},{9,25},{17,1},{25,9},{2,18},{10... | collective-permute-start | bytes 884744 | tf_op jit(solution)/shard_map/ppermute | solution.py:606
  245.5 8.5 %collective-permute-start.30 = (bf16[4,48,768]{2,1,0:T(8,128)(2,1)}, bf16[4,48,768]{2,1,0:T(8,128)(2,1)S(1)}, u32[]{:S(2)}, u32[]{:S(2)}) collective-permute-start(bf16[4,48,768]{2,1,0:T(8,128)(2,1)} %get-tuple-element.88), channel_id=1, source_target_pairs={{0,8},{8,0},{16,24},{24,16},{1,9},{9,1},{17,25},{25,17},{2,10},{10... | collective-permute-start | bytes 884744 | tf_op jit(solution)/shard_map/ppermute | solution.py:606
  259.1 5.9 %collective-permute-start.15 = (bf16[4,128,768]{2,1,0:T(8,128)(2,1)}, bf16[4,128,768]{2,1,0:T(8,128)(2,1)}, u32[]{:S(2)}, u32[]{:S(2)}) collective-permute-start(bf16[4,128,768]{2,1,0:T(8,128)(2,1)} %dynamic-slice_bitcast_fusion), channel_id=1, source_target_pairs={{0,1},{1,0},{2,3},{3,2},{4,5},{5,4},{6,7},{7,6},{8,9},{9,8},{10,11... | collective-permute-start | bytes 2359304 | tf_op jit(solution)/shard_map/ppermute | solution.py:788
  261.1 9.7 %collective-permute-start.31 = (bf16[2,48,768]{2,1,0:T(8,128)(2,1)}, bf16[2,48,768]{2,1,0:T(8,128)(2,1)S(1)}, u32[]{:S(2)}, u32[]{:S(2)}) collective-permute-start(bf16[2,48,768]{2,1,0:T(8,128)(2,1)} %get-tuple-element.90.refs_2_), channel_id=1, source_target_pairs={{0,2},{1,3},{2,0},{3,1},{4,6},{5,7},{6,4},{7,5},{8,10},{9,11},{10,... | collective-permute-start | bytes 442376 | tf_op jit(solution)/shard_map/ppermute | solution.py:614
  261.2 10.5 %collective-permute-start.32 = (bf16[2,48,768]{2,1,0:T(8,128)(2,1)S(1)}, bf16[2,48,768]{2,1,0:T(8,128)(2,1)S(1)}, u32[]{:S(2)}, u32[]{:S(2)}) collective-permute-start(bf16[2,48,768]{2,1,0:T(8,128)(2,1)S(1)} %copy-done.52), channel_id=1, source_target_pairs={{0,4},{1,5},{2,6},{3,7},{4,0},{5,1},{6,2},{7,3},{8,12},{9,13},{10,... | collective-permute-start | bytes 442376 | tf_op jit(solution)/shard_map/ppermute | solution.py:614
  264.7 52.5 %collective-permute-start.14 = (bf16[512,768]{1,0:T(8,128)(2,1)}, bf16[512,768]{1,0:T(8,128)(2,1)}, u32[]{:S(2)}, u32[]{:S(2)}) collective-permute-start(bf16[512,768]{1,0:T(8,128)(2,1)} %slice.138), channel_id=1, source_target_pairs={{0,1},{1,0},{2,3},{3,2},{4,5},{5,4},{6,7},{7,6},{8,9},{9,8},{10,11... | collective-permute-start | bytes 2359304 | tf_op jit(solution)/shard_map/ppermute | solution.py:825
  266.4 31.7 %collective-permute-start.16 = (bf16[128,768]{1,0:T(8,128)(2,1)S(1)}, bf16[128,768]{1,0:T(8,128)(2,1)S(1)}, u32[]{:S(2)}, u32[]{:S(2)}) collective-permute-start(bf16[128,768]{1,0:T(8,128)(2,1)S(1)} %get-tuple-element.141), channel_id=1, source_target_pairs={{0,2},{1,3},{2,0},{3,1},{4,6},{5,7},{6,4},{7,5},{8,10},{9,11},{10,... | collective-permute-start | bytes 589832 | tf_op jit(solution)/shard_map/ppermute | solution.py:614
  268.2 30.4 %collective-permute-start.17 = (bf16[128,768]{1,0:T(8,128)(2,1)S(1)}, bf16[128,768]{1,0:T(8,128)(2,1)S(1)}, u32[]{:S(2)}, u32[]{:S(2)}) collective-permute-start(bf16[128,768]{1,0:T(8,128)(2,1)S(1)} %get-tuple-element.143), channel_id=1, source_target_pairs={{0,4},{1,5},{2,6},{3,7},{4,0},{5,1},{6,2},{7,3},{8,12},{9,13},{10,... | collective-permute-start | bytes 589832 | tf_op jit(solution)/shard_map/ppermute | solution.py:614
  270.8 29.7 %collective-permute-start.18 = (bf16[128,768]{1,0:T(8,128)(2,1)S(1)}, bf16[128,768]{1,0:T(8,128)(2,1)S(1)}, u32[]{:S(2)}, u32[]{:S(2)}) collective-permute-start(bf16[128,768]{1,0:T(8,128)(2,1)S(1)} %get-tuple-element.142), channel_id=1, source_target_pairs={{0,6},{1,7},{2,4},{3,5},{4,2},{5,3},{6,0},{7,1},{8,14},{9,15},{10,... | collective-permute-start | bytes 589832 | tf_op jit(solution)/shard_map/ppermute | solution.py:614
  271.7 15.3 %collective-permute-start.33 = (bf16[2,48,768]{2,1,0:T(8,128)(2,1)S(1)}, bf16[2,48,768]{2,1,0:T(8,128)(2,1)S(1)}, u32[]{:S(2)}, u32[]{:S(2)}) collective-permute-start(bf16[2,48,768]{2,1,0:T(8,128)(2,1)S(1)} %copy-done.51), channel_id=1, source_target_pairs={{0,6},{1,7},{2,4},{3,5},{4,2},{5,3},{6,0},{7,1},{8,14},{9,15},{10,... | collective-permute-start | bytes 442376 | tf_op jit(solution)/shard_map/ppermute | solution.py:614
  289.6 13.9 %collective-permute-start.34 = (bf16[2,48,768]{2,1,0:T(8,128)(2,1)}, bf16[2,48,768]{2,1,0:T(8,128)(2,1)S(1)}, u32[]{:S(2)}, u32[]{:S(2)}) collective-permute-start(bf16[2,48,768]{2,1,0:T(8,128)(2,1)} %shard_map.236.refs_0_), channel_id=1, source_target_pairs={{0,2},{1,3},{2,0},{3,1},{4,6},{5,7},{6,4},{7,5},{8,10},{9,11},{10,... | collective-permute-start | bytes 442376 | tf_op jit(solution)/shard_map/ppermute | solution.py:614
  298.1 13.8 %collective-permute-start.35 = (bf16[2,48,768]{2,1,0:T(8,128)(2,1)}, bf16[2,48,768]{2,1,0:T(8,128)(2,1)S(1)}, u32[]{:S(2)}, u32[]{:S(2)}) collective-permute-start(bf16[2,48,768]{2,1,0:T(8,128)(2,1)} %shard_map.236.refs_0_), channel_id=1, source_target_pairs={{0,4},{1,5},{2,6},{3,7},{4,0},{5,1},{6,2},{7,3},{8,12},{9,13},{10,... | collective-permute-start | bytes 442376 | tf_op jit(solution)/shard_map/ppermute | solution.py:614
  298.6 13.3 %collective-permute-start.36 = (bf16[2,48,768]{2,1,0:T(8,128)(2,1)}, bf16[2,48,768]{2,1,0:T(8,128)(2,1)S(1)}, u32[]{:S(2)}, u32[]{:S(2)}) collective-permute-start(bf16[2,48,768]{2,1,0:T(8,128)(2,1)} %shard_map.236.refs_0_), channel_id=1, source_target_pairs={{0,6},{1,7},{2,4},{3,5},{4,2},{5,3},{6,0},{7,1},{8,14},{9,15},{10,... | collective-permute-start | bytes 442376 | tf_op jit(solution)/shard_map/ppermute | solution.py:614
  315.1 30.6 %collective-permute-start.37 = (bf16[4,48,768]{2,1,0:T(8,128)(2,1)}, bf16[4,48,768]{2,1,0:T(8,128)(2,1)S(1)}, u32[]{:S(2)}, u32[]{:S(2)}) collective-permute-start(bf16[4,48,768]{2,1,0:T(8,128)(2,1)} %get-tuple-element.93.x_ref), channel_id=1, source_target_pairs={{0,16},{8,24},{16,0},{24,8},{1,17},{9,25},{17,1},{25,9},{2,18},{10... | collective-permute-start | bytes 884744 | tf_op jit(solution)/shard_map/ppermute | solution.py:606
  315.7 30.0 %collective-permute-start.38 = (bf16[4,48,768]{2,1,0:T(8,128)(2,1)}, bf16[4,48,768]{2,1,0:T(8,128)(2,1)S(1)}, u32[]{:S(2)}, u32[]{:S(2)}) collective-permute-start(bf16[4,48,768]{2,1,0:T(8,128)(2,1)} %get-tuple-element.94.y_ref), channel_id=1, source_target_pairs={{0,8},{8,0},{16,24},{24,16},{1,9},{9,1},{17,25},{25,17},{2,10},{10... | collective-permute-start | bytes 884744 | tf_op jit(solution)/shard_map/ppermute | solution.py:606
  323.4 7.1 %collective-permute-start.19 = (bf16[128,768]{1,0:T(8,128)(2,1)S(1)}, bf16[128,768]{1,0:T(8,128)(2,1)S(1)}, u32[]{:S(2)}, u32[]{:S(2)}) collective-permute-start(bf16[128,768]{1,0:T(8,128)(2,1)S(1)} %get-tuple-element.125), channel_id=1, source_target_pairs={{0,6},{1,7},{2,0},{3,1},{4,2},{5,3},{6,4},{7,5},{8,14},{9,15},{10,... | collective-permute-start | bytes 589832 | tf_op jit(solution)/shard_map/ppermute | solution.py:674
  325.1 16.9 %collective-permute-start.20 = (bf16[128,768]{1,0:T(8,128)(2,1)S(1)}, bf16[128,768]{1,0:T(8,128)(2,1)S(1)}, u32[]{:S(2)}, u32[]{:S(2)}) collective-permute-start(bf16[128,768]{1,0:T(8,128)(2,1)S(1)} %get-tuple-element.124), channel_id=1, source_target_pairs={{0,4},{1,5},{2,6},{3,7},{4,0},{5,1},{6,2},{7,3},{8,12},{9,13},{10,... | collective-permute-start | bytes 589832 | tf_op jit(solution)/shard_map/ppermute | solution.py:674
  326.4 15.7 %collective-permute-start.21 = (bf16[128,768]{1,0:T(8,128)(2,1)S(1)}, bf16[128,768]{1,0:T(8,128)(2,1)S(1)}, u32[]{:S(2)}, u32[]{:S(2)}) collective-permute-start(bf16[128,768]{1,0:T(8,128)(2,1)S(1)} %get-tuple-element.123), channel_id=1, source_target_pairs={{0,2},{1,3},{2,4},{3,5},{4,6},{5,7},{6,0},{7,1},{8,10},{9,11},{10,... | collective-permute-start | bytes 589832 | tf_op jit(solution)/shard_map/ppermute | solution.py:674
  350.7 36.2 %collective-permute-start.45 = (bf16[4,4,576,256]{3,2,1,0:T(8,128)(2,1)}, bf16[4,4,576,256]{3,2,1,0:T(8,128)(2,1)}, u32[]{:S(2)}, u32[]{:S(2)}) collective-permute-start(bf16[4,4,576,256]{3,2,1,0:T(8,128)(2,1)} %shard_map.243.own_ref), channel_id=1, source_target_pairs={{0,1},{1,0},{2,3},{3,2},{4,5},{5,4},{6,7},{7,6},{8,9},{9,8},{10,11... | collective-permute-start | bytes 14155784 | tf_op jit(solution)/shard_map/ppermute | solution.py:606
  354.6 19.1 %collective-permute-start.39 = (bf16[2,4,48,768]{3,2,1,0:T(8,128)(2,1)S(1)}, bf16[2,4,48,768]{3,2,1,0:T(8,128)(2,1)S(1)}, u32[]{:S(2)}, u32[]{:S(2)}) collective-permute-start(bf16[2,4,48,768]{3,2,1,0:T(8,128)(2,1)S(1)} %copy-done.24), channel_id=1, source_target_pairs={{0,8},{8,0},{16,24},{24,16},{1,9},{9,1},{17,25},{25,17},{2,10},{10... | collective-permute-start | bytes 1769480 | tf_op jit(solution)/shard_map/ppermute | solution.py:606
  355.3 18.9 %collective-permute-start.42 = (bf16[2,4,48,768]{3,2,1,0:T(8,128)(2,1)S(1)}, bf16[2,4,48,768]{3,2,1,0:T(8,128)(2,1)S(1)}, u32[]{:S(2)}, u32[]{:S(2)}) collective-permute-start(bf16[2,4,48,768]{3,2,1,0:T(8,128)(2,1)S(1)} %copy-done.25), channel_id=1, source_target_pairs={{0,16},{8,24},{16,0},{24,8},{1,17},{9,25},{17,1},{25,9},{2,18},{10... | collective-permute-start | bytes 1769480 | tf_op jit(solution)/shard_map/ppermute | solution.py:606
  357.0 3.7 collective-permute-start.22
  360.7 4.5 %collective-permute-start.23 = (f32[16,128]{1,0:T(8,128)S(1)}, f32[16,128]{1,0:T(8,128)S(1)}, u32[]{:S(2)}, u32[]{:S(2)}) collective-permute-start(f32[16,128]{1,0:T(8,128)S(1)} %fusion.28), channel_id=1, source_target_pairs={{0,4},{1,5},{2,6},{3,7},{4,0},{5,1},{6,2},{7,3},{8,12},{9,13},{10,... | collective-permute-start | bytes 24584 | tf_op jit(solution)/shard_map/ppermute | solution.py:606
  366.4 3.7 collective-permute-start.25
  370.1 3.7 collective-permute-start.26
  371.6 5.1 %collective-permute-start.40 = (bf16[2,4,48,768]{3,2,1,0:T(8,128)(2,1)S(1)}, bf16[2,4,48,768]{3,2,1,0:T(8,128)(2,1)S(1)}, u32[]{:S(2)}, u32[]{:S(2)}) collective-permute-start(bf16[2,4,48,768]{3,2,1,0:T(8,128)(2,1)S(1)} %copy-done.24), channel_id=1, source_target_pairs={{0,1},{1,0},{2,3},{3,2},{4,5},{5,4},{6,7},{7,6},{8,9},{9,8},{10,11... | collective-permute-start | bytes 1769480 | tf_op jit(solution)/shard_map/ppermute | solution.py:606
  373.7 3.0 collective-permute-start.41
  374.2 3.2 collective-permute-start.44
  (72 other events, 393.0 us)
Sparse Core Ops, SparseCore 0:
  28.6 28.4 all-gather.5
  131.3 55.4 reduce-scatter.6
  193.2 27.9 reduce-scatter.4
  222.6 29.1 all-gather.7
  257.0 54.5 all-gather.9
